TPU v7x, 512 devices: a whole 4x8x8 slice. The times are simulated.
512 devices in a mesh: gy: 8 (over y_hi, core), gx: 8 (over y_lo, x), img: 8 (over z).
Axes of the slice: x: 4, y: 8 (y_hi: 4, y_lo: 2; y = y_hi * 2 + y_lo), z: 8, core: 2. Of those that a mesh axis runs over, the one named last changes fastest.
Arguments:
- inputs: bfloat16 [8, 64, 128, 512], P('img', 'gy', 'gx'), may hold values from -6 to 6
- cotangent: bfloat16 [8, 64, 128, 512], P('img', 'gy', 'gx'), may hold values from -6 to 6
- norm_gain: float32 [512], replicated, may hold values from 0.1 to 1.9
- w_qkv: bfloat16 [512, 1536], replicated, may hold values from -0.25 to 0.25
- w_out: bfloat16 [512, 512], replicated, may hold values from -0.25 to 0.25
- head_scale: float32 [8], replicated, may hold values from 2 to 10
Outputs:
- mixed: bfloat16 [8, 64, 128, 512], P('img', 'gy', 'gx')
- grad_input: bfloat16 [8, 64, 128, 512], P('img', 'gy', 'gx')
- grad_qkv: float32 [512, 1536], P(('gy', 'gx'))
- grad_out: float32 [512, 512], P(('gy', 'gx'))
All inputs are finite; a program needn't handle non-finite values.
Results may differ from a plain program's by a relative error of at most 0.012.
Values may be sent and summed in bfloat16 or wider, within the bound.
A program may use at most 64 MiB of HBM per device.

v0:
```python
import math

import jax
import jax.numpy as jnp
from jax import lax
from jax.sharding import PartitionSpec as P


def padded_2(x, sides, width):
    for axis, dim in sides:
        peers, length = (lax.axis_size(axis), x.shape[dim])
        up = [(i, (i + 1) % peers) for i in range(peers - 1)]
        down = [(j, i) for i, j in up]
        last = lax.slice_in_dim(x, length - width, length, axis=dim)
        first = lax.slice_in_dim(x, 0, width, axis=dim)
        before = lax.ppermute(last, axis, up)
        after = lax.ppermute(first, axis, down)
        x = jnp.concatenate([before, x, after], axis=dim)
    return x


def windows(values, axis_at):
    length = values.shape[axis_at] - 6
    blocks = length // 8
    widths = [(0, 0)] * values.ndim
    widths[axis_at] = (0, 2)
    padded = jnp.pad(values, widths)
    split_shape = values.shape[:axis_at] + (blocks, 8) + values.shape[axis_at + 1 :]
    leading = lax.slice_in_dim(padded, 0, length, axis=axis_at).reshape(split_shape)
    trailing = lax.slice_in_dim(padded, 8, length + 8, axis=axis_at).reshape(split_shape)
    trailing = lax.slice_in_dim(trailing, 0, 6, axis=axis_at + 1)
    return jnp.concatenate([leading, trailing], axis=axis_at + 1)


def unwindows(gradient, axis_at):
    blocks = gradient.shape[axis_at]
    length = blocks * 8
    merged = gradient.shape[:axis_at] + (length,) + gradient.shape[axis_at + 2 :]
    leading = lax.slice_in_dim(gradient, 0, 8, axis=axis_at + 1).reshape(merged)
    widths = [(0, 0)] * gradient.ndim
    widths[axis_at + 1] = (0, 2)
    trailing = jnp.pad(lax.slice_in_dim(gradient, 8, 14, axis=axis_at + 1), widths).reshape(merged)
    front_pad = [(0, 0)] * len(merged)
    front_pad[axis_at] = (0, 8)
    back_pad = [(0, 0)] * len(merged)
    back_pad[axis_at] = (8, 0)
    summed = jnp.pad(leading, front_pad) + jnp.pad(trailing, back_pad)
    return lax.slice_in_dim(summed, 0, length + 6, axis=axis_at)


def key_tiles(extended):
    both_win = windows(windows(extended, 0), 2)
    return both_win.transpose(0, 2, 1, 3, 4).reshape(-1, 196, extended.shape[-1])


def untile_keys(tiled, row_blocks, col_blocks):
    stacked = tiled.reshape(row_blocks, col_blocks, 14, 14, tiled.shape[-1]).transpose(
        0, 2, 1, 3, 4
    )
    return unwindows(unwindows(stacked, 2), 0)


def query_tiles(values):
    tile_rows, tile_cols, feats = values.shape
    shaped = values.reshape(tile_rows // 8, 8, tile_cols // 8, 8, feats)
    return shaped.transpose(0, 2, 1, 3, 4).reshape(-1, 64, feats)


def untile_queries(tiled, row_blocks, col_blocks):
    feats = tiled.shape[-1]
    shaped = tiled.reshape(row_blocks, col_blocks, 8, 8, feats).transpose(0, 2, 1, 3, 4)
    return shaped.reshape(row_blocks * 8, col_blocks * 8, feats)


def local_mask():
    query_ids = jnp.arange(64, dtype=jnp.int32)
    key_ids = jnp.arange(196, dtype=jnp.int32)
    row_gap = key_ids[None, :] // 14 - 3 - query_ids[:, None] // 8
    col_gap = key_ids[None, :] % 14 - 3 - query_ids[:, None] % 8
    return (jnp.abs(row_gap) <= 3) & (jnp.abs(col_gap) <= 3)


def tile_attention(queries, grad_attn, kv_ext, valid_ext, head_count):
    width = queries.shape[-1]
    head_dim = width // head_count
    q_tiles = query_tiles(queries)
    tiles = q_tiles.shape[0]
    q_heads = q_tiles.reshape(tiles, 64, head_count, head_dim)
    g_heads = query_tiles(grad_attn).reshape(tiles, 64, head_count, head_dim)
    keyed = key_tiles(kv_ext)
    k_heads = keyed[..., :width].reshape(tiles, 196, head_count, head_dim)
    v_heads = keyed[..., width:].reshape(tiles, 196, head_count, head_dim)
    allowed = local_mask()[None] & (key_tiles(valid_ext)[:, None, :, 0] > 0.5)
    scores = jnp.einsum("bqhd,bkhd->bhqk", q_heads, k_heads, preferred_element_type=jnp.float32)
    raw_weights = jnp.where(allowed[:, None], jnp.exp(scores), 0.0)
    probs = raw_weights / jnp.sum(raw_weights, -1, keepdims=True)
    probs_round = probs.astype(jnp.bfloat16)
    attended = jnp.einsum(
        "bhqk,bkhd->bqhd", probs_round, v_heads, preferred_element_type=jnp.float32
    ).astype(jnp.bfloat16)
    grad_probs = jnp.einsum("bqhd,bkhd->bhqk", g_heads, v_heads, preferred_element_type=jnp.float32)
    grad_v = jnp.einsum("bhqk,bqhd->bkhd", probs_round, g_heads, preferred_element_type=jnp.float32)
    centred = jnp.sum(probs * grad_probs, -1, keepdims=True)
    grad_scores = (probs * (grad_probs - centred)).astype(jnp.bfloat16)
    grad_q = jnp.einsum("bhqk,bkhd->bqhd", grad_scores, k_heads, preferred_element_type=jnp.float32)
    grad_k = jnp.einsum("bhqk,bqhd->bkhd", grad_scores, q_heads, preferred_element_type=jnp.float32)
    grad_kv = jnp.concatenate(
        [grad_k.reshape(tiles, 196, width), grad_v.reshape(tiles, 196, width)], -1
    )
    return (attended.reshape(tiles, 64, width), grad_q.reshape(tiles, 64, width), grad_kv)


def prepare(flat_x, norm_gain, w_qkv, head_scale):
    tokens_here, width = flat_x.shape
    head_count = head_scale.shape[0]
    head_dim = width // head_count
    x_float = flat_x.astype(jnp.float32)
    inv_rms = lax.rsqrt(jnp.mean(x_float * x_float, -1, keepdims=True) + 1e-06)
    normed = (x_float * inv_rms * norm_gain).astype(jnp.bfloat16)
    qkv = jnp.dot(normed, w_qkv, preferred_element_type=jnp.float32)
    q_raw = qkv[:, :width].reshape(tokens_here, head_count, head_dim)
    k_raw = qkv[:, width : 2 * width].reshape(tokens_here, head_count, head_dim)
    v_raw = qkv[:, 2 * width :]
    q_norm = lax.rsqrt(jnp.sum(q_raw * q_raw, -1, keepdims=True) + 1e-06)
    k_norm = lax.rsqrt(jnp.sum(k_raw * k_raw, -1, keepdims=True) + 1e-06)
    q_scaled = (
        (q_raw * q_norm * head_scale[:, None]).astype(jnp.bfloat16).reshape(tokens_here, width)
    )
    k_unit = (k_raw * k_norm).astype(jnp.bfloat16).reshape(tokens_here, width)
    kv_pair = jnp.concatenate([k_unit, v_raw.astype(jnp.bfloat16)], 1)
    return (x_float, inv_rms, normed, q_raw, k_raw, q_norm, k_norm, q_scaled, kv_pair)


def finish(flat_x, flat_dy, saved, attended, grad_qs, grad_kv, norm_gain, w_qkv, w_out, head_scale):
    x_float, inv_rms, normed, q_raw, k_raw, q_norm, k_norm = saved
    tokens_here, width = flat_x.shape
    head_count = head_scale.shape[0]
    head_dim = width // head_count
    grad_qs3 = grad_qs.reshape(tokens_here, head_count, head_dim)
    grad_ku3 = grad_kv[:, :width].reshape(tokens_here, head_count, head_dim)
    grad_q = head_scale[:, None] * (
        q_norm * grad_qs3
        - q_raw * q_norm * q_norm * q_norm * jnp.sum(q_raw * grad_qs3, -1, keepdims=True)
    )
    grad_k = k_norm * grad_ku3 - k_raw * k_norm * k_norm * k_norm * jnp.sum(
        k_raw * grad_ku3, -1, keepdims=True
    )
    grad_act = jnp.concatenate(
        [
            grad_q.reshape(tokens_here, width),
            grad_k.reshape(tokens_here, width),
            grad_kv[:, width:],
        ],
        1,
    ).astype(jnp.bfloat16)
    grad_normed = jnp.dot(grad_act, w_qkv.T, preferred_element_type=jnp.float32)
    part_qkv = jnp.dot(normed.T, grad_act, preferred_element_type=jnp.float32)
    scaled_grad = grad_normed * norm_gain
    grad_input = (
        flat_dy.astype(jnp.float32)
        + inv_rms * scaled_grad
        - x_float * inv_rms * inv_rms * inv_rms * jnp.mean(x_float * scaled_grad, -1, keepdims=True)
    ).astype(jnp.bfloat16)
    mixed = (x_float + jnp.dot(attended, w_out, preferred_element_type=jnp.float32)).astype(
        jnp.bfloat16
    )
    part_out = jnp.dot(attended.T, flat_dy, preferred_element_type=jnp.float32)
    return (mixed, grad_input, part_qkv, part_out)


def per_device(inputs, cotangent, norm_gain, w_qkv, w_out, head_scale):
    tile_rows, tile_cols, width = (inputs.shape[1], inputs.shape[2], inputs.shape[3])
    head_count = head_scale.shape[0]
    tokens_here = tile_rows * tile_cols
    row_blocks = tile_rows // 8
    col_blocks = tile_cols // 8
    flat_x = inputs.reshape(tokens_here, width)
    flat_dy = cotangent.reshape(tokens_here, width)
    prepared = prepare(flat_x, norm_gain, w_qkv, head_scale)
    q_scaled, kv_pair = (prepared[7], prepared[8])
    kv_grid = kv_pair.reshape(tile_rows, tile_cols, 2 * width)
    kv_ext = padded_2(kv_grid, (("gy", 0), ("gx", 1)), 3)
    grad_attn = jnp.dot(flat_dy, w_out.T, preferred_element_type=jnp.float32).astype(jnp.bfloat16)
    row_ids = lax.axis_index("gy") * tile_rows + jnp.arange(tile_rows + 6, dtype=jnp.int32) - 3
    col_ids = lax.axis_index("gx") * tile_cols + jnp.arange(tile_cols + 6, dtype=jnp.int32) - 3
    row_inside = (row_ids >= 0) & (row_ids < tile_rows * lax.axis_size("gy"))
    col_inside = (col_ids >= 0) & (col_ids < tile_cols * lax.axis_size("gx"))
    valid_ext = (row_inside[:, None] & col_inside[None, :]).astype(jnp.float32)[:, :, None]
    out_tiles, dq_tiles, dkv_tiles = tile_attention(
        q_scaled.reshape(tile_rows, tile_cols, width),
        grad_attn.reshape(tile_rows, tile_cols, width),
        kv_ext,
        valid_ext,
        head_count,
    )
    attended = untile_queries(out_tiles, row_blocks, col_blocks).reshape(tokens_here, width)
    grad_qs = untile_queries(dq_tiles, row_blocks, col_blocks).reshape(tokens_here, width)
    grad_ext = untile_keys(dkv_tiles, row_blocks, col_blocks)
    col_sides = jnp.concatenate([grad_ext[:, :3], grad_ext[:, tile_cols + 3 :]], axis=1)
    from_cols = padded_2(col_sides.astype(jnp.bfloat16), (("gx", 1),), 3).astype(col_sides.dtype)
    inner = grad_ext[:, 3 : tile_cols + 3]
    inner = inner.at[:, :3].add(from_cols[:, :3]).at[:, tile_cols - 3 :].add(from_cols[:, 9:])
    row_sides = jnp.concatenate([inner[:3], inner[tile_rows + 3 :]], axis=0)
    from_rows = padded_2(row_sides.astype(jnp.bfloat16), (("gy", 0),), 3).astype(row_sides.dtype)
    middle = inner[3 : tile_rows + 3]
    middle = middle.at[:3].add(from_rows[:3]).at[tile_rows - 3 :].add(from_rows[9:])
    grad_kv = middle.reshape(tokens_here, 2 * width)
    mixed, grad_input, part_qkv, part_out = finish(
        flat_x,
        flat_dy,
        prepared[:7],
        attended,
        grad_qs,
        grad_kv,
        norm_gain,
        w_qkv,
        w_out,
        head_scale,
    )
    rows_mine = width // (lax.axis_size("gy") * lax.axis_size("gx"))
    offset = lax.axis_index(("gy", "gx")) * rows_mine
    total_qkv, total_out = lax.psum((part_qkv, part_out), ("gy", "gx", "img"))
    mine_qkv = lax.dynamic_slice_in_dim(total_qkv, offset, rows_mine, 0)
    mine_out = lax.dynamic_slice_in_dim(total_out, offset, rows_mine, 0)
    factor = 1.0 / math.sqrt(
        lax.axis_size("img") * lax.axis_size("gy") * tile_rows * lax.axis_size("gx") * tile_cols
    )
    shape_out = (1, tile_rows, tile_cols, width)
    return (
        mixed.reshape(shape_out),
        grad_input.reshape(shape_out),
        mine_qkv * factor,
        mine_out * factor,
    )


def solution(mesh):
    in_specs = (P("img", "gy", "gx", None), P("img", "gy", "gx", None), P(), P(), P(), P())
    out_specs = (
        P("img", "gy", "gx", None),
        P("img", "gy", "gx", None),
        P(("gy", "gx"), None),
        P(("gy", "gx"), None),
    )
    return jax.shard_map(
        per_device, mesh=mesh, in_specs=in_specs, out_specs=out_specs, check_vma=False
    )
```

profile of v0, /device:TPU:6, one launch (start us, length us, event | category | flops | bytes accessed | tf_op | source)
XLA Modules:
  0.0 420.3 jit_solution(16551727543224826385)
XLA Ops:
  11.7 1.6 pad_maximum_fusion.16
  14.6 3.7 collective-permute-start
  28.3 3.4 collective-permute-start.2
  31.7 2.4 collective-permute-start.3
  37.2 4.2 collective-permute-done.3
  49.0 2.8 fusion.4
  51.8 3.0 convolution_bitcast_fusion
  60.1 2.3 copy.78
  63.9 2.3 copy.76
  66.2 1.6 concatenate.70
  67.8 2.2 maximum_bitcast_fusion
  74.2 2.1 copy.66
  78.4 1.9 copy.73
  80.7 1.9 collective-permute-start.4
  82.6 4.1 collective-permute-start.5
  87.8 4.0 collective-permute-done.5
  93.4 2.5 scatter-add.14
  99.1 1.9 collective-permute-start.6
  103.4 1.7 collective-permute-done.7
  108.7 1.8 copy.84
  110.5 1.7 fusion
  112.2 1.8 copy.85
  115.1 3.2 fusion.30
  122.0 288.7 %all-reduce.13.cloned.1.call-done = (f32[512,1536]{1,0:T(8,128)}, f32[512,512]{1,0:T(8,128)}) async-done(((f32[512,1536]{1,0:T(8,128)}, f32[512,512]{1,0:T(8,128)}), (f32[512,1536]{1,0:T(8,128)}, f32[512,512]{1,0:T(8,128)})) %all-reduce.13.cloned.1.call-update) | async-done | bytes 4194320 | tf_op jit(solution)/shard_map/psum | solution.py:222
  (180 shorter events, 58.6 us)
Async XLA Ops:
  7.2 403.5 %all-reduce.13.cloned.1.call-start = ((), (), s32[]{:S(2)}) async-start(), calls=%async_computation | async-start | bytes 8388608 | tf_op jit(solution)/shard_map/psum | solution.py:222
  11.3 8.2 %copy-start.33 = (f32[8]{0:T(128)S(1)}, f32[8]{0:T(128)}, u32[]{:S(2)}) copy-start(f32[8]{0:T(128)} %param.19) | copy-start | bytes 100
  11.6 10.8 %copy-start.7 = (f32[128,512]{1,0:T(8,128)}, f32[128,512]{1,0:T(8,128)S(1)}, u32[]{:S(2)}) copy-start(f32[128,512]{1,0:T(8,128)S(1)} %copy.51) | copy-start | bytes 786436
  11.7 11.6 %copy-start.9 = (bf16[512,512]{1,0:T(8,128)(2,1)S(1)}, bf16[512,512]{1,0:T(8,128)(2,1)}, u32[]{:S(2)}) copy-start(bf16[512,512]{1,0:T(8,128)(2,1)} %param.18) | copy-start | bytes 1572868
  13.3 14.0 %collective-permute-start.1 = (bf16[3,16,1024]{2,1,0:T(8,128)(2,1)}, bf16[3,16,1024]{2,1,0:T(8,128)(2,1)}, u32[]{:S(2)}, u32[]{:S(2)}) collective-permute-start(bf16[3,16,1024]{2,1,0:T(8,128)(2,1)} %bitcast.6), channel_id=1, source_target_pairs={{64,0},{128,64},{192,128},{256,192},{320,256},{384,320},{448,384},... | collective-permute-start | bytes 294920 | tf_op jit(solution)/shard_map/ppermute | solution.py:17
  14.6 12.7 %collective-permute-start = (bf16[3,16,1024]{2,1,0:T(8,128)(2,1)}, bf16[3,16,1024]{2,1,0:T(8,128)(2,1)}, u32[]{:S(2)}, u32[]{:S(2)}) collective-permute-start(bf16[3,16,1024]{2,1,0:T(8,128)(2,1)} %bitcast.3), channel_id=1, source_target_pairs={{0,64},{64,128},{128,192},{192,256},{256,320},{320,384},{384,448},... | collective-permute-start | bytes 294920 | tf_op jit(solution)/shard_map/ppermute | solution.py:16
  20.6 5.0 %copy-start.5 = (f32[128,512]{0,1:T(8,128)}, f32[128,512]{0,1:T(8,128)S(1)}, u32[]{:S(2)}) copy-start(f32[128,512]{0,1:T(8,128)S(1)} %copy.57) | copy-start | bytes 786436
  28.3 8.9 %collective-permute-start.2 = (bf16[14,3,1024]{2,1,0:T(4,128)(2,1)S(1)}, bf16[14,3,1024]{2,1,0:T(4,128)(2,1)S(1)}, u32[]{:S(2)}, u32[]{:S(2)}) collective-permute-start(bf16[14,3,1024]{2,1,0:T(4,128)(2,1)S(1)} %get-tuple-element.66), channel_id=1, source_target_pairs={{0,8},{8,16},{16,24},{24,32},{32,40},{40,48},{48,56},{1,9},{9,17},... | collective-permute-start | bytes 258056 | tf_op jit(solution)/shard_map/ppermute | solution.py:16
  31.7 9.7 %collective-permute-start.3 = (bf16[14,3,1024]{2,1,0:T(4,128)(2,1)S(1)}, bf16[14,3,1024]{2,1,0:T(4,128)(2,1)S(1)}, u32[]{:S(2)}, u32[]{:S(2)}) collective-permute-start(bf16[14,3,1024]{2,1,0:T(4,128)(2,1)S(1)} %get-tuple-element.67), channel_id=1, source_target_pairs={{8,0},{16,8},{24,16},{32,24},{40,32},{48,40},{56,48},{9,1},{17,9},... | collective-permute-start | bytes 258056 | tf_op jit(solution)/shard_map/ppermute | solution.py:17
  80.7 11.2 %copy-start.22 = (bf16[14,3,1024]{2,1,0:T(4,128)(2,1)}, bf16[14,3,1024]{2,1,0:T(4,128)(2,1)S(1)}, u32[]{:S(2)}) copy-start(bf16[14,3,1024]{2,1,0:T(4,128)(2,1)S(1)} %get-tuple-element.58) | copy-start | bytes 258052
  80.7 11.2 %copy-start.23 = (bf16[14,3,1024]{2,1,0:T(4,128)(2,1)}, bf16[14,3,1024]{2,1,0:T(4,128)(2,1)S(1)}, u32[]{:S(2)}) copy-start(bf16[14,3,1024]{2,1,0:T(4,128)(2,1)S(1)} %get-tuple-element.59) | copy-start | bytes 258052
  80.7 7.1 %collective-permute-start.4 = (bf16[14,3,1024]{2,1,0:T(4,128)(2,1)S(1)}, bf16[14,3,1024]{2,1,0:T(4,128)(2,1)S(1)}, u32[]{:S(2)}, u32[]{:S(2)}) collective-permute-start(bf16[14,3,1024]{2,1,0:T(4,128)(2,1)S(1)} %get-tuple-element.58), channel_id=1, source_target_pairs={{0,8},{8,16},{16,24},{24,32},{32,40},{40,48},{48,56},{1,9},{9,17},... | collective-permute-start | bytes 258056 | tf_op jit(solution)/shard_map/ppermute | solution.py:16
  82.6 9.2 %collective-permute-start.5 = (bf16[14,3,1024]{2,1,0:T(4,128)(2,1)S(1)}, bf16[14,3,1024]{2,1,0:T(4,128)(2,1)S(1)}, u32[]{:S(2)}, u32[]{:S(2)}) collective-permute-start(bf16[14,3,1024]{2,1,0:T(4,128)(2,1)S(1)} %get-tuple-element.59), channel_id=1, source_target_pairs={{8,0},{16,8},{24,16},{32,24},{40,32},{48,40},{56,48},{9,1},{17,9},... | collective-permute-start | bytes 258056 | tf_op jit(solution)/shard_map/ppermute | solution.py:17
  87.8 4.1 copy-start.27
  96.0 6.3 %copy-start.6 = (f32[128,512]{0,1:T(8,128)S(1)}, f32[128,512]{0,1:T(8,128)}, u32[]{:S(2)}) copy-start(f32[128,512]{0,1:T(8,128)} %copy-done.5) | copy-start | bytes 786436
  96.0 6.3 %copy-start.19 = (f32[128,8,64]{0,2,1:T(8,128)S(1)}, f32[128,8,64]{0,2,1:T(8,128)}, u32[]{:S(2)}) copy-start(f32[128,8,64]{0,2,1:T(8,128)} %copy.73) | copy-start | bytes 786436
  99.1 4.3 %collective-permute-start.6 = (bf16[3,16,1024]{2,1,0:T(8,128)(2,1)}, bf16[3,16,1024]{2,1,0:T(8,128)(2,1)}, u32[]{:S(2)}, u32[]{:S(2)}) collective-permute-start(bf16[3,16,1024]{2,1,0:T(8,128)(2,1)} %get-tuple-element.64), channel_id=1, source_target_pairs={{0,64},{64,128},{128,192},{192,256},{256,320},{320,384},{384,448},... | collective-permute-start | bytes 294920 | tf_op jit(solution)/shard_map/ppermute | solution.py:16
  101.0 4.1 collective-permute-start.7
  103.3 4.5 %copy-start.2 = (f32[128,1536]{1,0:T(8,128)S(1)}, f32[128,1536]{1,0:T(8,128)}, u32[]{:S(2)}) copy-start(f32[128,1536]{1,0:T(8,128)} %copy-done.1) | copy-start | bytes 2359300
  103.3 4.5 %copy-start.20 = (f32[128,512]{1,0:T(8,128)S(1)}, f32[128,512]{1,0:T(8,128)}, u32[]{:S(2)}) copy-start(f32[128,512]{1,0:T(8,128)} %copy.68) | copy-start | bytes 786436
  103.3 4.5 %copy-start.21 = (f32[128,512]{1,0:T(8,128)S(1)}, f32[128,512]{1,0:T(8,128)}, u32[]{:S(2)}) copy-start(f32[128,512]{1,0:T(8,128)} %copy.74) | copy-start | bytes 786436
  107.8 6.2 %copy-start.8 = (f32[128,512]{1,0:T(8,128)S(1)}, f32[128,512]{1,0:T(8,128)}, u32[]{:S(2)}) copy-start(f32[128,512]{1,0:T(8,128)} %copy-done.7) | copy-start | bytes 786436
  108.7 5.3 %copy-start.4 = (f32[8,16,1024]{2,1,0:T(8,128)S(1)}, f32[8,16,1024]{2,1,0:T(8,128)}, u32[]{:S(2)}) copy-start(f32[8,16,1024]{2,1,0:T(8,128)} %copy-done.3) | copy-start | bytes 1572868
  108.7 6.4 %copy-start.14 = (bf16[128,512]{1,0:T(8,128)(2,1)S(1)}, bf16[128,512]{1,0:T(8,128)(2,1)}, u32[]{:S(2)}) copy-start(bf16[128,512]{1,0:T(8,128)(2,1)} %copy-done.13) | copy-start | bytes 393220
  (19 other events, 32.7 us)
Sparse Core Ops, SparseCore 0:
  118.5 292.1 all-reduce.12
where the time goes:
time: 424 us; the launch traced here: 420 us
  waiting for transfers between devices  300 us (71%)
  local copies, waits for them, and re-layouts  39.6 us (9%)
  other arithmetic  26.1 us (6%)
  matrix products  20.1 us (5%)
  starting transfers between devices  20 us (5%)
  between operations  14.8 us (3%)
    psum x1, waiting for transfers between devices, per_device(): total_qkv, total_out = lax.psum((part_qkv, part_out), ('gy', 'gx', 'img'))  289 us
    ppermute x4, starting transfers between devices, padded_2(): before = lax.ppermute(last, axis, up)  10.9 us
    ppermute x4, waiting for transfers between devices, padded_2(): after = lax.ppermute(first, axis, down)  9.92 us
    ppermute x4, starting transfers between devices, padded_2(): after = lax.ppermute(first, axis, down)  9.11 us
  transfers between devices with their start and end apart: 9, of which 5 were waited for; matrix products, arithmetic and copies ran while one was open for 4% of the time, Pallas kernels for 0%

commit v1 on v0

--- a/solution.py
+++ b/solution.py
@@ -3,7 +3,287 @@
 import jax
 import jax.numpy as jnp
 from jax import lax
+from jax.experimental import pallas as pl
+from jax.experimental.pallas import tpu as pltpu
 from jax.sharding import PartitionSpec as P
+
+F32, BF16 = jnp.float32, jnp.bfloat16
+
+
+class Links:
+    def __init__(self, send, recv):
+        self.send, self.recv, self.used, self.all = send, recv, 0, []
+
+    def start(self, src, dst, device):
+        copy = pltpu.make_async_remote_copy(
+            src_ref=src,
+            dst_ref=dst,
+            send_sem=self.send.at[self.used],
+            recv_sem=self.recv.at[self.used],
+            device_id=device,
+            device_id_type=pl.DeviceIdType.MESH,
+        )
+        copy.start()
+        self.used += 1
+        self.all.append(copy)
+        return copy
+
+    def drain(self):
+        for copy in self.all:
+            copy.wait_send()
+
+
+class Place:
+    def __init__(self):
+        gy, gx, self.z = lax.axis_index("gy"), lax.axis_index("gx"), lax.axis_index("img")
+        self.gy, self.gx = gy, gx
+        self.ngy, self.ngx, self.nz = (lax.axis_size(a) for a in ("gy", "gx", "img"))
+        self.nx = self.ngx // 2
+        self.ny = self.ngy
+        self.core, self.x = gy % 2, gx % self.nx
+        self.y = (gy // 2) * 2 + gx // self.nx
+
+    def other_core(self):
+        return (self.gy + 1 - 2 * self.core, self.gx, self.z)
+
+    def x_peer(self, k):
+        to = (self.x + k) % self.nx
+        return to, (self.gy, self.gx - self.x + to, self.z)
+
+    def y_peer(self, k):
+        to = (self.y + k) % self.ny
+        return to, ((to // 2) * 2 + self.core, (to % 2) * self.nx + self.x, self.z)
+
+    def z_peer(self, k):
+        to = (self.z + k) % self.nz
+        return to, (self.gy, self.gx, to)
+
+    def reduce_peers(self):
+        return (
+            [self.other_core()]
+            + [self.x_peer(k)[1] for k in range(1, self.nx)]
+            + [self.y_peer(k)[1] for k in range(1, self.ny)]
+            + [self.z_peer(k)[1] for k in range(1, self.nz)]
+        )
+
+
+def enter(devices):
+    barrier = pltpu.get_barrier_semaphore()
+    for device in devices:
+        pl.semaphore_signal(barrier, inc=1, device_id=device, device_id_type=pl.DeviceIdType.MESH)
+    return lambda: pl.semaphore_wait(barrier, len(devices))
+
+
+def reduce_scratch(nx, ny, nz):
+    v = pltpu.VMEM
+    return dict(
+        r0a=v((ny, nx, 4, 16, 128), BF16),
+        r0b=v((ny, 2, 8, 16, 128), BF16),
+        s1a=v((ny, nx, 4, 16, 128), BF16),
+        s1b=v((ny, 2, 8, 16, 128), BF16),
+        rxa=v((nx - 1, ny, 4, 16, 128), BF16),
+        s2a=v((ny, 4, 16, 128), BF16),
+        rya=v((ny - 1, 4, 16, 128), BF16),
+        ta=v((nz, 8, 128), F32),
+        rza=v((nz - 1, 8, 128), F32),
+        ga=v((nz, 8, 128), F32),
+        ryb=v((ny - 1, 8, 16, 128), BF16),
+        rzb=v((nz - 1, ny, 16, 128), BF16),
+        syb=v((nz, 16, 128), BF16),
+        szb=v((ny, 16, 128), BF16),
+        r2z=v((nz - 1, 16, 128), BF16),
+        r2y=v((ny - 1, 16, 128), BF16),
+        ub=v((nx, 8, 128), F32),
+        r3x=v((nx - 1, 8, 128), F32),
+        gb=v((nz, 8, 128), F32),
+    )
+
+
+def reduce_count(nx, ny, nz):
+    return 2 + 2 * (nx - 1) + 3 * (ny - 1) + 5 * (nz - 1)
+
+
+def core_add(s1, own, got):
+    def add(i, _):
+        s1[i] = (own[i].astype(F32) + got[i].astype(F32)).astype(BF16)
+        return 0
+
+    lax.fori_loop(0, s1.shape[0], add, 0)
+
+
+def reduce_tail(p, links, b, own_a, own_b, first_a, first_b, factor):
+    nx, ny, nz = p.nx, p.ny, p.nz
+    first_a.wait_recv()
+    core_add(b["s1a"], own_a, b["r0a"])
+    xs = []
+    for k in range(1, nx):
+        to, device = p.x_peer(k)
+        xs.append(links.start(b["s1a"].at[:, to], b["rxa"].at[k - 1], device))
+
+    first_b.wait_recv()
+    core_add(b["s1b"], own_b, b["r0b"])
+    ys, zs = [], []
+    for k in range(1, max(ny, nz)):
+        if k < ny:
+            to, device = p.y_peer(k)
+            ys.append(links.start(b["s1b"].at[to, 0], b["ryb"].at[k - 1], device))
+        if k < nz:
+            to, device = p.z_peer(k)
+            zs.append(links.start(b["s1b"].at[:, 1, to], b["rzb"].at[k - 1], device))
+
+    for c in xs:
+        c.wait_recv()
+
+    def add_x(i, _):
+        total = b["s1a"][i, p.x].astype(F32)
+        for k in range(nx - 1):
+            total += b["rxa"][k, i].astype(F32)
+        b["s2a"][i] = total.astype(BF16)
+        return 0
+
+    lax.fori_loop(0, ny, add_x, 0)
+    y2 = []
+    for k in range(1, ny):
+        to, device = p.y_peer(k)
+        y2.append(links.start(b["s2a"].at[to], b["rya"].at[k - 1], device))
+
+    for c in ys:
+        c.wait_recv()
+
+    def add_y(i, _):
+        total = b["s1b"][p.y, 0, i].astype(F32)
+        for k in range(ny - 1):
+            total += b["ryb"][k, i].astype(F32)
+        b["syb"][i] = total.astype(BF16)
+        return 0
+
+    lax.fori_loop(0, nz, add_y, 0)
+    z3 = []
+    for k in range(1, nz):
+        to, device = p.z_peer(k)
+        z3.append(links.start(b["syb"].at[to], b["r2z"].at[k - 1], device))
+
+    for c in zs:
+        c.wait_recv()
+
+    def add_z(i, _):
+        total = b["s1b"][i, 1, p.z].astype(F32)
+        for k in range(nz - 1):
+            total += b["rzb"][k, i].astype(F32)
+        b["szb"][i] = total.astype(BF16)
+        return 0
+
+    lax.fori_loop(0, ny, add_z, 0)
+    y3 = []
+    for k in range(1, ny):
+        to, device = p.y_peer(k)
+        y3.append(links.start(b["szb"].at[to], b["r2y"].at[k - 1], device))
+
+    for c in y2:
+        c.wait_recv()
+    total = b["s2a"][p.y].astype(F32)
+    for k in range(ny - 1):
+        total += b["rya"][k].astype(F32)
+    b["ta"][0:4] = total[:, 0:8]
+    b["ta"][4:8] = total[:, 8:16]
+    z2 = []
+    for k in range(1, nz):
+        to, device = p.z_peer(k)
+        z2.append(links.start(b["ta"].at[to], b["rza"].at[k - 1], device))
+
+    for c in z3:
+        c.wait_recv()
+    low = b["syb"][p.z].astype(F32)
+    for k in range(nz - 1):
+        low += b["r2z"][k].astype(F32)
+    for c in y3:
+        c.wait_recv()
+    high = b["szb"][p.y].astype(F32)
+    for k in range(ny - 1):
+        high += b["r2y"][k].astype(F32)
+    b["ub"][0] = low[0:8]
+    b["ub"][1] = low[8:16]
+    b["ub"][2] = high[0:8]
+    b["ub"][3] = high[8:16]
+    x3 = []
+    for k in range(1, nx):
+        to, device = p.x_peer(k)
+        x3.append(links.start(b["ub"].at[to], b["r3x"].at[k - 1], device))
+
+    for c in z2:
+        c.wait_recv()
+    total = b["ta"][p.z]
+    for k in range(nz - 1):
+        total += b["rza"][k]
+    b["ga"][p.z] = total * factor
+    last = []
+    for k in range(1, nz):
+        to, device = p.z_peer(k)
+        last.append(links.start(b["ga"].at[p.z], b["ga"].at[p.z], device))
+
+    for c in x3:
+        c.wait_recv()
+    total = b["ub"][p.x]
+    for k in range(nx - 1):
+        total += b["r3x"][k]
+    b["gb"][p.z] = total * factor
+    for k in range(1, nz):
+        to, device = p.z_peer(k)
+        last.append(links.start(b["gb"].at[p.z], b["gb"].at[p.z], device))
+    for c in last:
+        c.wait_recv()
+
+
+def write_rows(b, qkv_ref, out_ref):
+    for t in range(4):
+        lanes = slice(t * 128, t * 128 + 128)
+        qkv_ref[:, lanes] = b["ga"][t]
+        out_ref[:, lanes] = b["ga"][4 + t]
+    for t in range(8):
+        qkv_ref[:, 512 + t * 128 : 640 + t * 128] = b["gb"][t]
+
+
+def reduce_call(part_a, part_b, factor):
+    nx, ny, nz = lax.axis_size("gx") // 2, lax.axis_size("gy"), lax.axis_size("img")
+    scratch = reduce_scratch(nx, ny, nz)
+    names = list(scratch)
+    count = reduce_count(nx, ny, nz)
+
+    def kernel(a_ref, b_ref, qkv_ref, out_ref, *rest):
+        b = dict(zip(names, rest))
+        links = Links(*rest[len(names) :])
+        p = Place()
+        wait = enter(p.reduce_peers())
+        wait()
+        first_a = links.start(a_ref.at[1 - p.core], b["r0a"], p.other_core())
+        first_b = links.start(b_ref.at[1 - p.core], b["r0b"], p.other_core())
+        reduce_tail(p, links, b, a_ref.at[p.core], b_ref.at[p.core], first_a, first_b, factor)
+        write_rows(b, qkv_ref, out_ref)
+        links.drain()
+
+    vm = pl.BlockSpec(memory_space=pltpu.VMEM)
+    return pl.pallas_call(
+        kernel,
+        out_shape=(jax.ShapeDtypeStruct((8, 1536), F32), jax.ShapeDtypeStruct((8, 512), F32)),
+        in_specs=[vm, vm],
+        out_specs=(vm, vm),
+        scratch_shapes=[scratch[n] for n in names]
+        + [pltpu.SemaphoreType.DMA((count,)), pltpu.SemaphoreType.DMA((count,))],
+        compiler_params=pltpu.CompilerParams(
+            collective_id=1, has_side_effects=True, vmem_limit_bytes=48 * 1024 * 1024
+        ),
+        cost_estimate=pl.CostEstimate(flops=10**7, bytes_accessed=4 * 10**6, transcendentals=0),
+        name="reduce",
+    )(part_a, part_b)
+
+
+def fold_parts(part_qkv, part_out):
+    ny, nx = lax.axis_size("gy"), lax.axis_size("gx") // 2
+    split = lambda a: a.reshape(ny // 2, 2, 2, nx, 8, a.shape[-1]).transpose(1, 0, 2, 3, 4, 5)
+    both = jnp.concatenate([split(part_qkv[:, :512]), split(part_out)], axis=4)
+    part_a = both.reshape(2, ny, nx, 16, 4, 128).swapaxes(3, 4).astype(BF16)
+    rest = split(part_qkv[:, 512:]).reshape(2, ny, nx // 2, 16, 8, 128)
+    return (part_a, rest.swapaxes(3, 4).astype(BF16))
 
 
 def padded_2(x, sides, width):
@@ -217,20 +497,16 @@
         w_out,
         head_scale,
     )
-    rows_mine = width // (lax.axis_size("gy") * lax.axis_size("gx"))
-    offset = lax.axis_index(("gy", "gx")) * rows_mine
-    total_qkv, total_out = lax.psum((part_qkv, part_out), ("gy", "gx", "img"))
-    mine_qkv = lax.dynamic_slice_in_dim(total_qkv, offset, rows_mine, 0)
-    mine_out = lax.dynamic_slice_in_dim(total_out, offset, rows_mine, 0)
     factor = 1.0 / math.sqrt(
         lax.axis_size("img") * lax.axis_size("gy") * tile_rows * lax.axis_size("gx") * tile_cols
     )
+    mine_qkv, mine_out = reduce_call(*fold_parts(part_qkv, part_out), factor)
     shape_out = (1, tile_rows, tile_cols, width)
     return (
         mixed.reshape(shape_out),
         grad_input.reshape(shape_out),
-        mine_qkv * factor,
-        mine_out * factor,
+        mine_qkv,
+        mine_out,
     )
 
 

time: 424 us -> 175 us (0.41)
  waiting for transfers between devices: 300 us -> 0.74 us
  Pallas kernels: 0 us -> 41.3 us
  between operations: 14.8 us -> 1.52 us
  local copies, waits for them, and re-layouts: 39.6 us -> 52.3 us
  starting transfers between devices: 20 us -> 26.5 us
    psum x1 -> x0, waiting for transfers between devices: 289 us -> none  [per_device(): total_qkv, total_out = lax.psum((part_qkv, part_out), ('gy', 'gx', 'img'))]
    pallas_call x0 -> x1, Pallas kernels: none -> 41.3 us  [reduce_call(): pl.pallas_call(kernel, out_shape=(jax.ShapeDtypeStruct((8, 1536), F32), j...]
    ppermute x4, waiting for transfers between devices: 9.92 us -> 0.01 us  [padded_2(): after = lax.ppermute(first, axis, down)]
    ppermute x4, starting transfers between devices: 10.9 us -> 16.6 us  [padded_2(): before = lax.ppermute(last, axis, up)]
  transfers between devices with their start and end apart: 9 -> 8, of which waited for: 5 -> 1; matrix products, arithmetic and copies ran while one was open for 4% -> 16% of each run, Pallas kernels for 0% -> 0%
where the time goes in v1:
time: 175 us; the launch traced here: 172 us
  local copies, waits for them, and re-layouts  52.3 us (30%)
  Pallas kernels  41.3 us (24%)
  other arithmetic  28.7 us (16%)
  starting transfers between devices  26.5 us (15%)
  matrix products  21.2 us (12%)
    pallas_call x1, Pallas kernels, reduce_call(): pl.pallas_call(kernel, out_shape=(jax.ShapeDtypeStruct((8, 1536), F32), j...  41.3 us
    ppermute x4, starting transfers between devices, padded_2(): before = lax.ppermute(last, axis, up)  16.6 us
    ppermute x4, starting transfers between devices, padded_2(): after = lax.ppermute(first, axis, down)  9.9 us
    scatter-add x2, local copies, waits for them, and re-layouts, per_device(): inner.at[:, :3].add(from_cols[:, :3]).at[:, tile_cols - 3:]  6.67 us
    unnamed x83, local copies, waits for them, and re-layouts  6.58 us
  transfers between devices with their start and end apart: 8, of which 1 were waited for; matrix products, arithmetic and copies ran while one was open for 16% of the time, Pallas kernels for 0%

profile of v1, /device:TPU:6, one launch (start us, length us, event | category | flops | bytes accessed | tf_op | source)
XLA Modules:
  0.0 172.2 jit_solution(12632328232739488647)
XLA Ops:
  8.6 3.7 %collective-permute-start = (bf16[3,16,1024]{2,1,0:T(8,128)(2,1)}, bf16[3,16,1024]{2,1,0:T(8,128)(2,1)}, u32[]{:S(2)}, u32[]{:S(2)}) collective-permute-start(bf16[3,16,1024]{2,1,0:T(8,128)(2,1)} %bitcast.3), channel_id=1, source_target_pairs={{0,64},{64,128},{128,192},{192,256},{256,320},{320,384},{384,448},... | collective-permute-start | bytes 294920 | tf_op jit(solution)/shard_map/ppermute | solution.py:296
  22.3 2.7 %collective-permute-start.3 = (bf16[14,3,1024]{2,1,0:T(4,128)(2,1)S(1)}, bf16[14,3,1024]{2,1,0:T(4,128)(2,1)S(1)}, u32[]{:S(2)}, u32[]{:S(2)}) collective-permute-start(bf16[14,3,1024]{2,1,0:T(4,128)(2,1)S(1)} %get-tuple-element.69), channel_id=1, source_target_pairs={{8,0},{16,8},{24,16},{32,24},{40,32},{48,40},{56,48},{9,1},{17,9},... | collective-permute-start | bytes 258056 | tf_op jit(solution)/shard_map/ppermute | solution.py:297
  25.1 5.2 %collective-permute-start.2 = (bf16[14,3,1024]{2,1,0:T(4,128)(2,1)S(1)}, bf16[14,3,1024]{2,1,0:T(4,128)(2,1)S(1)}, u32[]{:S(2)}, u32[]{:S(2)}) collective-permute-start(bf16[14,3,1024]{2,1,0:T(4,128)(2,1)S(1)} %get-tuple-element.68), channel_id=1, source_target_pairs={{0,8},{8,16},{16,24},{24,32},{32,40},{40,48},{48,56},{1,9},{9,17},... | collective-permute-start | bytes 258056 | tf_op jit(solution)/shard_map/ppermute | solution.py:296
  39.0 2.7 %fusion.5 = bf16[2,64,8,64]{1,3,2,0:T(8,128)(2,1)} fusion(bf16[2,196,8,64]{1,3,2,0:T(8,128)(2,1)S(1)} %bitcast.175, f32[2,8,64,196]{3,2,1,0:T(8,128)} %fusion.3), kind=kOutput, calls=%fused_computation.20 | convolution fusion | flops 26158276 | bytes 1335296 | tf_op jit(solution)/shard_map/bhqk,bkhd->bqhd/dot_general | solution.py:378
  41.7 3.0 %convolution_bitcast_fusion = f32[2,196,8,64]{1,3,2,0:T(8,128)} fusion(bf16[2,64,8,64]{1,3,2,0:T(8,128)(2,1)S(1)} %copy-done.27, f32[2,8,64,196]{3,2,1,0:T(8,128)} %fusion.3), kind=kOutput, calls=%fused_computation.12 | convolution fusion | flops 26092740 | bytes 1736704 | tf_op jit(solution)/shard_map/bhqk,bqhd->bkhd/dot_general | solution.py:382
  46.0 2.3 %copy.83 = f32[2,196,8,64]{3,2,0,1:T(8,128)S(1)} copy(f32[2,196,8,64]{1,3,2,0:T(8,128)} %convolution_bitcast_fusion) | data formatting | bytes 1605632 | tf_op jit(solution)/shard_map/bhqk,bqhd->bkhd/transpose | solution.py:382
  49.8 3.0 %multiply_reduce_fusion = (f32[2,8,64]{2,1,0:T(8,128)S(1)}, f32[2,8,64,196]{3,2,1,0:T(8,128)}) fusion(f32[2,8,64,196]{3,2,1,0:T(8,128)} %fusion.50, bf16[2,64,8,64]{1,3,2,0:T(8,128)(2,1)S(1)} %copy.80, bf16[2,196,8,64]{1,3,2,0:T(8,128)(2,1)} %bitcast.165, pred[2,64,196]{2,1,0:T(8,128)(4,1)S(1)} %broadcast_and_fusion), kind=kOutput, calls=%fused_computation.29 | convolution fusion | flops 26493124 | bytes 2167296 | tf_op jit(solution)/shard_map/div | solution.py:376
  56.2 2.3 %copy.81 = f32[2,196,8,64]{3,2,0,1:T(8,128)S(1)} copy(f32[2,196,8,64]{1,3,2,0:T(8,128)} %convolution_bitcast_fusion.1) | data formatting | bytes 1605632 | tf_op jit(solution)/shard_map/bhqk,bqhd->bkhd/transpose | solution.py:386
  60.1 2.2 %maximum_bitcast_fusion = f32[1,14,2,14,1024]{4,2,3,1,0:T(2,128)S(1)} fusion(f32[1,2,14,14,512]{4,1,3,2,0:T(2,128)} %concatenate.75, f32[1,2,14,14,512]{4,1,3,2,0:T(2,128)} %concatenate.74), kind=kLoop, calls=%fused_computation.8 | loop fusion | flops 401408 | bytes 3211264 | tf_op jit(solution)/shard_map/transpose | solution.py:337
  68.8 4.6 %collective-permute-start.5 = (bf16[14,3,1024]{2,1,0:T(4,128)(2,1)}, bf16[14,3,1024]{2,1,0:T(4,128)(2,1)}, u32[]{:S(2)}, u32[]{:S(2)}) collective-permute-start(bf16[14,3,1024]{2,1,0:T(4,128)(2,1)} %get-tuple-element.61), channel_id=1, source_target_pairs={{8,0},{16,8},{24,16},{32,24},{40,32},{48,40},{56,48},{9,1},{17,9},... | collective-permute-start | bytes 258056 | tf_op jit(solution)/shard_map/ppermute | solution.py:297
  73.4 4.0 %collective-permute-start.4 = (bf16[14,3,1024]{2,1,0:T(4,128)(2,1)}, bf16[14,3,1024]{2,1,0:T(4,128)(2,1)}, u32[]{:S(2)}, u32[]{:S(2)}) collective-permute-start(bf16[14,3,1024]{2,1,0:T(4,128)(2,1)} %get-tuple-element.60), channel_id=1, source_target_pairs={{0,8},{8,16},{16,24},{24,32},{32,40},{40,48},{48,56},{1,9},{9,17},... | collective-permute-start | bytes 258056 | tf_op jit(solution)/shard_map/ppermute | solution.py:296
  77.4 2.0 %copy.71 = f32[2,64,8,64]{3,2,1,0:T(8,128)} copy(f32[2,64,8,64]{1,3,2,0:T(8,128)} %convolution_bitcast_fusion.2) | data formatting | bytes 524288 | tf_op jit(solution)/shard_map/bhqk,bkhd->bqhd/transpose | solution.py:385
  79.4 1.9 %reshape_reshape.23 = f32[1,2,8,8,512]{4,3,2,1,0:T(8,128)} reshape(f32[2,64,8,64]{3,2,1,0:T(8,128)} %copy.71) | data formatting | bytes 524288 | tf_op jit(solution)/shard_map/reshape;reshape | solution.py:351
  83.2 1.9 %copy.78 = f32[128,8,64]{0,2,1:T(8,128)} copy(f32[128,8,64]{2,1,0:T(8,128)} %reshape_reshape_reshape.7) | data formatting | bytes 524288 | tf_op jit(solution)/shard_map/reshape;reshape;reshape | solution.py:419
  86.9 2.0 %fusion.6 = bf16[128,512]{1,0:T(8,128)(2,1)} fusion(bf16[128,512]{1,0:T(8,128)(2,1)} %bitcast.185, bf16[512,512]{1,0:T(8,128)(2,1)} %param.18, bf16[128,512]{1,0:T(8,128)(2,1)S(1)} %bitcast.177), kind=kOutput, calls=%fused_computation.23 | convolution fusion | flops 67305472 | bytes 917504 | tf_op jit(solution)/shard_map/dot_general | solution.py:444
  88.9 1.8 %fusion.1 = f32[128,8,64]{0,2,1:T(8,128)} fusion(f32[128,8,64]{0,2,1:T(8,128)} %bitcast.173, f32[128,8,64]{0,2,1:T(8,128)} %copy.78), kind=kOutput, calls=%fused_computation.1 | output fusion | flops 66623 | bytes 786432 | tf_op jit(solution)/shard_map/mul | solution.py:423
  91.7 2.0 %fusion.28 = f32[14,3,1024]{2,1,0:T(4,128)} fusion(f32[8,22,1024]{2,1,0:T(8,128)S(1)} %fusion.9, f32[8,22,1024]{2,1,0:T(8,128)S(1)} %pad_bitcast_fusion.1, bf16[14,3,1024]{2,1,0:T(4,128)(2,1)} %collective-permute-done.5, bf16[14,3,1024]{2,1,0:T(4,128)(2,1)} %get-tuple-element.60, bf16[14,3,1024]{2,1,0:T(4,128)(2,1)} %get-tuple-element.61, ...), kind=kLoop, calls=%fused_computation.81 | loop fusion | flops 430080 | bytes 1957888 | tf_op jit(solution)/shard_map/add | solution.py:482
  93.7 3.7 %scatter-add.14 = f32[14,16,1024]{2,1,0:T(8,128)} dynamic-update-slice(f32[14,16,1024]{2,1,0:T(8,128)} %fusion.7, f32[14,3,1024]{2,1,0:T(4,128)} %fusion.28, s32[]{:T(128)} %constant.181.clone.1, s32[]{:T(128)} %constant.181.clone.1, s32[]{:T(128)} %constant.181.clone.1) | dynamic-update-slice | bytes 344068 | tf_op jit(solution)/shard_map/scatter-add | solution.py:482
  98.7 3.0 %scatter-add.15 = f32[14,16,1024]{2,1,0:T(8,128)} dynamic-update-slice(f32[14,16,1024]{2,1,0:T(8,128)} %scatter-add.14, f32[14,3,1024]{2,1,0:T(4,128)S(1)} %slice_add_fusion, s32[]{:T(128)} %constant.181.clone.1, s32[]{:T(128)} %constant.194.clone.1, s32[]{:T(128)} %constant.181.clone.1) | dynamic-update-slice | bytes 344068 | tf_op jit(solution)/shard_map/scatter-add | solution.py:482
  105.0 3.7 %collective-permute-start.6 = (bf16[3,16,1024]{2,1,0:T(8,128)(2,1)}, bf16[3,16,1024]{2,1,0:T(8,128)(2,1)}, u32[]{:S(2)}, u32[]{:S(2)}) collective-permute-start(bf16[3,16,1024]{2,1,0:T(8,128)(2,1)} %get-tuple-element.66), channel_id=1, source_target_pairs={{0,64},{64,128},{128,192},{192,256},{256,320},{320,384},{384,448},... | collective-permute-start | bytes 294920 | tf_op jit(solution)/shard_map/ppermute | solution.py:296
  114.4 1.9 %copy.89 = f32[128,512]{0,1:T(8,128)} copy(f32[128,512]{1,0:T(8,128)} %get-tuple-element.59) | data formatting | bytes 524288 | tf_op jit(solution)/shard_map/mul | solution.py:426
  116.3 1.7 fusion
  118.0 1.8 %copy.90 = f32[128,512]{1,0:T(8,128)} copy(f32[128,512]{0,1:T(8,128)} %bitcast.193) | data formatting | bytes 524288 | tf_op jit(solution)/shard_map/mul | solution.py:425
  128.7 41.3 %reduce.10 = (f32[8,1536]{1,0:T(8,128)S(1)}, f32[8,512]{1,0:T(8,128)S(1)}) custom-call(bf16[2,8,4,4,16,128]{5,4,3,2,1,0:T(8,128)(2,1)S(1)} %bitcast.159, bf16[2,8,2,8,16,128]{5,4,3,2,1,0:T(8,128)(2,1)S(1)} %bitcast.160), custom_call_target="tpu_custom_call" | custom-call | flops 10000000 | bytes 4000000 | tf_op jit(solution)/shard_map/reduce/pallas_call | solution.py:265
  (199 shorter events, 66.3 us)
Async XLA Ops:
  5.6 10.5 %copy-start.13 = (f32[128,512]{1,0:T(8,128)}, f32[128,512]{1,0:T(8,128)S(1)}, u32[]{:S(2)}) copy-start(f32[128,512]{1,0:T(8,128)S(1)} %copy.56) | copy-start | bytes 786436
  5.7 15.7 %copy-start.19 = (bf16[128,512]{1,0:T(8,128)(2,1)}, bf16[128,512]{1,0:T(8,128)(2,1)S(1)}, u32[]{:S(2)}) copy-start(bf16[128,512]{1,0:T(8,128)(2,1)S(1)} %get-tuple-element.63) | copy-start | bytes 393220
  5.7 11.3 %copy-start.38 = (f32[8]{0:T(128)S(1)}, f32[8]{0:T(128)}, u32[]{:S(2)}) copy-start(f32[8]{0:T(128)} %param.19) | copy-start | bytes 100
  5.7 12.4 %copy-start.15 = (bf16[512,512]{1,0:T(8,128)(2,1)S(1)}, bf16[512,512]{1,0:T(8,128)(2,1)}, u32[]{:S(2)}) copy-start(bf16[512,512]{1,0:T(8,128)(2,1)} %param.18) | copy-start | bytes 1572868
  7.3 14.1 %collective-permute-start.1 = (bf16[3,16,1024]{2,1,0:T(8,128)(2,1)}, bf16[3,16,1024]{2,1,0:T(8,128)(2,1)}, u32[]{:S(2)}, u32[]{:S(2)}) collective-permute-start(bf16[3,16,1024]{2,1,0:T(8,128)(2,1)} %bitcast.6), channel_id=1, source_target_pairs={{64,0},{128,64},{192,128},{256,192},{320,256},{384,320},{448,384},... | collective-permute-start | bytes 294920 | tf_op jit(solution)/shard_map/ppermute | solution.py:297
  8.6 12.8 %collective-permute-start = (bf16[3,16,1024]{2,1,0:T(8,128)(2,1)}, bf16[3,16,1024]{2,1,0:T(8,128)(2,1)}, u32[]{:S(2)}, u32[]{:S(2)}) collective-permute-start(bf16[3,16,1024]{2,1,0:T(8,128)(2,1)} %bitcast.3), channel_id=1, source_target_pairs={{0,64},{64,128},{128,192},{192,256},{256,320},{320,384},{384,448},... | collective-permute-start | bytes 294920 | tf_op jit(solution)/shard_map/ppermute | solution.py:296
  22.3 10.4 %collective-permute-start.3 = (bf16[14,3,1024]{2,1,0:T(4,128)(2,1)S(1)}, bf16[14,3,1024]{2,1,0:T(4,128)(2,1)S(1)}, u32[]{:S(2)}, u32[]{:S(2)}) collective-permute-start(bf16[14,3,1024]{2,1,0:T(4,128)(2,1)S(1)} %get-tuple-element.69), channel_id=1, source_target_pairs={{8,0},{16,8},{24,16},{32,24},{40,32},{48,40},{56,48},{9,1},{17,9},... | collective-permute-start | bytes 258056 | tf_op jit(solution)/shard_map/ppermute | solution.py:297
  25.1 8.4 %collective-permute-start.2 = (bf16[14,3,1024]{2,1,0:T(4,128)(2,1)S(1)}, bf16[14,3,1024]{2,1,0:T(4,128)(2,1)S(1)}, u32[]{:S(2)}, u32[]{:S(2)}) collective-permute-start(bf16[14,3,1024]{2,1,0:T(4,128)(2,1)S(1)} %get-tuple-element.68), channel_id=1, source_target_pairs={{0,8},{8,16},{16,24},{24,32},{32,40},{40,48},{48,56},{1,9},{9,17},... | collective-permute-start | bytes 258056 | tf_op jit(solution)/shard_map/ppermute | solution.py:296
  68.8 22.9 %collective-permute-start.5 = (bf16[14,3,1024]{2,1,0:T(4,128)(2,1)}, bf16[14,3,1024]{2,1,0:T(4,128)(2,1)}, u32[]{:S(2)}, u32[]{:S(2)}) collective-permute-start(bf16[14,3,1024]{2,1,0:T(4,128)(2,1)} %get-tuple-element.61), channel_id=1, source_target_pairs={{8,0},{16,8},{24,16},{32,24},{40,32},{48,40},{56,48},{9,1},{17,9},... | collective-permute-start | bytes 258056 | tf_op jit(solution)/shard_map/ppermute | solution.py:297
  73.4 18.3 %collective-permute-start.4 = (bf16[14,3,1024]{2,1,0:T(4,128)(2,1)}, bf16[14,3,1024]{2,1,0:T(4,128)(2,1)}, u32[]{:S(2)}, u32[]{:S(2)}) collective-permute-start(bf16[14,3,1024]{2,1,0:T(4,128)(2,1)} %get-tuple-element.60), channel_id=1, source_target_pairs={{0,8},{8,16},{16,24},{24,32},{32,40},{40,48},{48,56},{1,9},{9,17},... | collective-permute-start | bytes 258056 | tf_op jit(solution)/shard_map/ppermute | solution.py:296
  79.4 7.4 %copy-start.16 = (bf16[1,8,16,512]{3,2,1,0:T(8,128)(2,1)S(1)}, bf16[1,8,16,512]{3,2,1,0:T(8,128)(2,1)}, u32[]{:S(2)}) copy-start(bf16[1,8,16,512]{3,2,1,0:T(8,128)(2,1)} %param.14) | copy-start | bytes 393220
  97.3 11.4 %copy-start.24 = (bf16[1,8,16,512]{3,2,1,0:T(8,128)(2,1)S(1)}, bf16[1,8,16,512]{3,2,1,0:T(8,128)(2,1)}, u32[]{:S(2)}) copy-start(bf16[1,8,16,512]{3,2,1,0:T(8,128)(2,1)} %param.15) | copy-start | bytes 393220
  97.3 11.4 %copy-start.32 = (bf16[512,128]{1,0:T(8,128)(2,1)S(1)}, bf16[512,128]{1,0:T(8,128)(2,1)}, u32[]{:S(2)}) copy-start(bf16[512,128]{1,0:T(8,128)(2,1)} %copy.91) | copy-start | bytes 393220
  98.7 11.1 %copy-start.28 = (f32[128,8,64]{0,2,1:T(8,128)S(1)}, f32[128,8,64]{0,2,1:T(8,128)}, u32[]{:S(2)}) copy-start(f32[128,8,64]{0,2,1:T(8,128)} %fusion.1) | copy-start | bytes 786436
  101.7 8.9 %copy-start.1 = (f32[14,16,1024]{2,1,0:T(8,128)S(1)}, f32[14,16,1024]{2,1,0:T(8,128)}, u32[]{:S(2)}) copy-start(f32[14,16,1024]{2,1,0:T(8,128)} %scatter-add.15) | copy-start | bytes 2752516
  103.8 6.9 %collective-permute-start.7 = (bf16[3,16,1024]{2,1,0:T(8,128)(2,1)}, bf16[3,16,1024]{2,1,0:T(8,128)(2,1)}, u32[]{:S(2)}, u32[]{:S(2)}) collective-permute-start(bf16[3,16,1024]{2,1,0:T(8,128)(2,1)} %get-tuple-element.67), channel_id=1, source_target_pairs={{64,0},{128,64},{192,128},{256,192},{320,256},{384,320},{448,384},... | collective-permute-start | bytes 294920 | tf_op jit(solution)/shard_map/ppermute | solution.py:297
  105.0 5.7 %collective-permute-start.6 = (bf16[3,16,1024]{2,1,0:T(8,128)(2,1)}, bf16[3,16,1024]{2,1,0:T(8,128)(2,1)}, u32[]{:S(2)}, u32[]{:S(2)}) collective-permute-start(bf16[3,16,1024]{2,1,0:T(8,128)(2,1)} %get-tuple-element.66), channel_id=1, source_target_pairs={{0,64},{64,128},{128,192},{192,256},{256,320},{320,384},{384,448},... | collective-permute-start | bytes 294920 | tf_op jit(solution)/shard_map/ppermute | solution.py:296
  114.4 6.4 %copy-start.30 = (bf16[128,512]{1,0:T(8,128)(2,1)}, bf16[128,512]{1,0:T(8,128)(2,1)S(1)}, u32[]{:S(2)}) copy-start(bf16[128,512]{1,0:T(8,128)(2,1)S(1)} %get-tuple-element.58) | copy-start | bytes 393220
  114.4 6.4 %copy-start.17 = (bf16[1,8,16,512]{3,2,1,0:T(8,128)(2,1)S(1)}, bf16[1,8,16,512]{3,2,1,0:T(8,128)(2,1)}, u32[]{:S(2)}) copy-start(bf16[1,8,16,512]{3,2,1,0:T(8,128)(2,1)} %param.14) | copy-start | bytes 393220
  114.4 6.4 %copy-start.31 = (bf16[128,512]{1,0:T(8,128)(2,1)S(1)}, bf16[128,512]{1,0:T(8,128)(2,1)}, u32[]{:S(2)}) copy-start(bf16[128,512]{1,0:T(8,128)(2,1)} %slice.385) | copy-start | bytes 393220
  114.4 6.5 %copy-start.37 = (f32[512]{0:T(512)S(1)}, f32[512]{0:T(512)}, u32[]{:S(2)}) copy-start(f32[512]{0:T(512)} %param.16) | copy-start | bytes 6148
  128.7 41.4 %copy-start.25 = (bf16[1,8,16,512]{3,2,1,0:T(8,128)(2,1)S(1)}, bf16[1,8,16,512]{3,2,1,0:T(8,128)(2,1)}, u32[]{:S(2)}) copy-start(bf16[1,8,16,512]{3,2,1,0:T(8,128)(2,1)} %param.15) | copy-start | bytes 393220
  128.7 41.4 %copy-start.33 = (f32[128,512]{1,0:T(8,128)S(1)}, f32[128,512]{1,0:T(8,128)}, u32[]{:S(2)}) copy-start(f32[128,512]{1,0:T(8,128)} %get-tuple-element.77) | copy-start | bytes 786436
  128.7 41.4 %copy-start.36 = (f32[128]{0:T(128)S(1)}, f32[128]{0:T(128)}, u32[]{:S(2)}) copy-start(f32[128]{0:T(128)} %copy-done.35) | copy-start | bytes 1540
  (24 other events, 61.7 us)

commit v2 on v1

v2 whole, which is shorter than its diff:
```python
import math

import jax
import jax.numpy as jnp
from jax import lax
from jax.experimental import pallas as pl
from jax.experimental.pallas import tpu as pltpu
from jax.sharding import PartitionSpec as P

F32, BF16 = jnp.float32, jnp.bfloat16


class Links:
    def __init__(self, send, recv):
        self.send, self.recv, self.used, self.all = send, recv, 0, []

    def start(self, src, dst, device):
        copy = pltpu.make_async_remote_copy(
            src_ref=src,
            dst_ref=dst,
            send_sem=self.send.at[self.used],
            recv_sem=self.recv.at[self.used],
            device_id=device,
            device_id_type=pl.DeviceIdType.MESH,
        )
        copy.start()
        self.used += 1
        self.all.append(copy)
        return copy

    def drain(self):
        for copy in self.all:
            copy.wait_send()


class Place:
    def __init__(self):
        gy, gx, self.z = lax.axis_index("gy"), lax.axis_index("gx"), lax.axis_index("img")
        self.gy, self.gx = gy, gx
        self.ngy, self.ngx, self.nz = (lax.axis_size(a) for a in ("gy", "gx", "img"))
        self.nx = self.ngx // 2
        self.ny = self.ngy
        self.core, self.x = gy % 2, gx % self.nx
        self.y = (gy // 2) * 2 + gx // self.nx

    def other_core(self):
        return (self.gy + 1 - 2 * self.core, self.gx, self.z)

    def x_peer(self, k):
        to = (self.x + k) % self.nx
        return to, (self.gy, self.gx - self.x + to, self.z)

    def y_peer(self, k):
        to = (self.y + k) % self.ny
        return to, ((to // 2) * 2 + self.core, (to % 2) * self.nx + self.x, self.z)

    def z_peer(self, k):
        to = (self.z + k) % self.nz
        return to, (self.gy, self.gx, to)

    def reduce_peers(self):
        return (
            [self.other_core()]
            + [self.x_peer(k)[1] for k in range(1, self.nx)]
            + [self.y_peer(k)[1] for k in range(1, self.ny)]
            + [self.z_peer(k)[1] for k in range(1, self.nz)]
        )


def enter(devices):
    barrier = pltpu.get_barrier_semaphore()
    for device in devices:
        pl.semaphore_signal(barrier, inc=1, device_id=device, device_id_type=pl.DeviceIdType.MESH)
    return lambda: pl.semaphore_wait(barrier, len(devices))


def reduce_scratch(nx, ny, nz):
    v = pltpu.VMEM
    return dict(
        r0a=v((ny, nx, 4, 16, 128), BF16),
        r0b=v((ny, 2, 8, 16, 128), BF16),
        s1a=v((ny, nx, 4, 16, 128), BF16),
        s1b=v((ny, 2, 8, 16, 128), BF16),
        rxa=v((nx - 1, ny, 4, 16, 128), BF16),
        s2a=v((ny, 4, 16, 128), BF16),
        rya=v((ny - 1, 4, 16, 128), BF16),
        ta=v((nz, 8, 128), F32),
        rza=v((nz - 1, 8, 128), F32),
        ga=v((nz, 8, 128), F32),
        ryb=v((ny - 1, 8, 16, 128), BF16),
        rzb=v((nz - 1, ny, 16, 128), BF16),
        syb=v((nz, 16, 128), BF16),
        szb=v((ny, 16, 128), BF16),
        r2z=v((nz - 1, 16, 128), BF16),
        r2y=v((ny - 1, 16, 128), BF16),
        ub=v((nx, 8, 128), F32),
        r3x=v((nx - 1, 8, 128), F32),
        gb=v((nz, 8, 128), F32),
    )


def reduce_count(nx, ny, nz):
    return 2 + 2 * (nx - 1) + 3 * (ny - 1) + 5 * (nz - 1)


def core_add(s1, own, got):
    def add(i, _):
        s1[i] = (own[i].astype(F32) + got[i].astype(F32)).astype(BF16)
        return 0

    lax.fori_loop(0, s1.shape[0], add, 0)


def start_a(p, links, b, first_a):
    first_a.wait_recv()
    core_add(b["s1a"], b["own_a"], b["r0a"])
    xs = []
    for k in range(1, p.nx):
        to, device = p.x_peer(k)
        xs.append(links.start(b["s1a"].at[:, to], b["rxa"].at[k - 1], device))
    return xs


def reduce_tail(p, links, b, first_b, xs, finish, factor):
    nx, ny, nz = p.nx, p.ny, p.nz
    first_b.wait_recv()
    core_add(b["s1b"], b["own_b"], b["r0b"])
    ys, zs = [], []
    for k in range(1, max(ny, nz)):
        if k < ny:
            to, device = p.y_peer(k)
            ys.append(links.start(b["s1b"].at[to, 0], b["ryb"].at[k - 1], device))
        if k < nz:
            to, device = p.z_peer(k)
            zs.append(links.start(b["s1b"].at[:, 1, to], b["rzb"].at[k - 1], device))
    finish()

    for c in xs:
        c.wait_recv()

    def add_x(i, _):
        total = b["s1a"][i, p.x].astype(F32)
        for k in range(nx - 1):
            total += b["rxa"][k, i].astype(F32)
        b["s2a"][i] = total.astype(BF16)
        return 0

    lax.fori_loop(0, ny, add_x, 0)
    y2 = []
    for k in range(1, ny):
        to, device = p.y_peer(k)
        y2.append(links.start(b["s2a"].at[to], b["rya"].at[k - 1], device))

    for c in ys:
        c.wait_recv()

    def add_y(i, _):
        total = b["s1b"][p.y, 0, i].astype(F32)
        for k in range(ny - 1):
            total += b["ryb"][k, i].astype(F32)
        b["syb"][i] = total.astype(BF16)
        return 0

    lax.fori_loop(0, nz, add_y, 0)
    z3 = []
    for k in range(1, nz):
        to, device = p.z_peer(k)
        z3.append(links.start(b["syb"].at[to], b["r2z"].at[k - 1], device))

    for c in zs:
        c.wait_recv()

    def add_z(i, _):
        total = b["s1b"][i, 1, p.z].astype(F32)
        for k in range(nz - 1):
            total += b["rzb"][k, i].astype(F32)
        b["szb"][i] = total.astype(BF16)
        return 0

    lax.fori_loop(0, ny, add_z, 0)
    y3 = []
    for k in range(1, ny):
        to, device = p.y_peer(k)
        y3.append(links.start(b["szb"].at[to], b["r2y"].at[k - 1], device))

    for c in y2:
        c.wait_recv()
    total = b["s2a"][p.y].astype(F32)
    for k in range(ny - 1):
        total += b["rya"][k].astype(F32)
    b["ta"][0:4] = total[:, 0:8]
    b["ta"][4:8] = total[:, 8:16]
    z2 = []
    for k in range(1, nz):
        to, device = p.z_peer(k)
        z2.append(links.start(b["ta"].at[to], b["rza"].at[k - 1], device))

    for c in z3:
        c.wait_recv()
    low = b["syb"][p.z].astype(F32)
    for k in range(nz - 1):
        low += b["r2z"][k].astype(F32)
    for c in y3:
        c.wait_recv()
    high = b["szb"][p.y].astype(F32)
    for k in range(ny - 1):
        high += b["r2y"][k].astype(F32)
    b["ub"][0] = low[0:8]
    b["ub"][1] = low[8:16]
    b["ub"][2] = high[0:8]
    b["ub"][3] = high[8:16]
    x3 = []
    for k in range(1, nx):
        to, device = p.x_peer(k)
        x3.append(links.start(b["ub"].at[to], b["r3x"].at[k - 1], device))

    for c in z2:
        c.wait_recv()
    total = b["ta"][p.z]
    for k in range(nz - 1):
        total += b["rza"][k]
    b["ga"][p.z] = total * factor
    last = []
    for k in range(1, nz):
        to, device = p.z_peer(k)
        last.append(links.start(b["ga"].at[p.z], b["ga"].at[p.z], device))

    for c in x3:
        c.wait_recv()
    total = b["ub"][p.x]
    for k in range(nx - 1):
        total += b["r3x"][k]
    b["gb"][p.z] = total * factor
    for k in range(1, nz):
        to, device = p.z_peer(k)
        last.append(links.start(b["gb"].at[p.z], b["gb"].at[p.z], device))
    for c in last:
        c.wait_recv()


def write_rows(b, qkv_ref, out_ref):
    for t in range(4):
        lanes = slice(t * 128, t * 128 + 128)
        qkv_ref[:, lanes] = b["ga"][t]
        out_ref[:, lanes] = b["ga"][4 + t]
    for t in range(8):
        qkv_ref[:, 512 + t * 128 : 640 + t * 128] = b["gb"][t]


def dot(a, b, dims=((1,), (0,))):
    return lax.dot_general(a, b, (dims, ((), ())), preferred_element_type=F32)


TURN = ((1,), (1,))
FIRST = ((0,), (0,))


def iota(shape, dim):
    return lax.broadcasted_iota(jnp.int32, shape, dim)


def edge_tokens(j):
    side = j & 31
    side_token = jnp.where((side >> 3) < 3, (side & 7) * 16 + (side >> 3) + 13 * ((j >> 5) & 1), -1)
    corner = (j - 64) >> 4
    down, across = (j >> 2) & 3, j & 3
    token = (down + 5 * (corner >> 1)) * 16 + across + 13 * (corner & 1)
    corner_token = jnp.where((down < 3) & (across < 3), token, -1)
    return jnp.where(j < 64, side_token, corner_token)


def halo_place(j):
    row = jnp.where(j < 48, (j >> 4) - 3, (j >> 4) + 5)
    col = j & 15
    side = j & 31
    is_side = (j >= 96) & (j < 160)
    row = jnp.where(is_side, side & 7, row)
    col = jnp.where(is_side, (side >> 3) + jnp.where(j < 128, -3, 16), col)
    corner = (j - 160) >> 4
    down, across = (j >> 2) & 3, j & 3
    is_corner = j >= 160
    row = jnp.where(is_corner, down + jnp.where(corner < 2, -3, 8), row)
    col = jnp.where(is_corner, across + jnp.where((corner & 1) == 0, -3, 16), col)
    filled = jnp.where(is_side, side >> 3, jnp.where(is_corner, jnp.maximum(down, across), 0))
    return row, col, filled < 3


def near(row, col, shape):
    query = iota(shape, 1)
    return (jnp.abs(row - (query >> 4)) <= 3) & (jnp.abs(col - (query & 15)) <= 3)


def twice(a):
    return jnp.concatenate([a, a], axis=1)


def head_sum(a, ones):
    top = a.astype(BF16)
    rest = (a - top.astype(F32)).astype(BF16)
    return dot(top, ones) + dot(rest, ones)


def pick(a):
    return jnp.concatenate([a[0:64, 0:128], a[64:128, 128:256]], axis=0)


BLOCKS = (
    (0, 48, 48, -1, 0),
    (48, 48, 0, 1, 0),
    (96, 32, 128, 0, -1),
    (128, 32, 96, 0, 1),
    (160, 16, 208, -1, -1),
    (176, 16, 192, -1, 1),
    (192, 16, 176, 1, -1),
    (208, 16, 160, 1, 1),
)


def block_call(x, dy, gain, w_qkv, w_out, head_scale, factor):
    nx, ny, nz = lax.axis_size("gx") // 2, lax.axis_size("gy"), lax.axis_size("img")
    v = pltpu.VMEM
    scratch = reduce_scratch(nx, ny, nz)
    scratch.update(
        own_a=v((ny, nx, 4, 16, 128), F32),
        own_b=v((ny, 2, 8, 16, 128), F32),
        s0a=v((ny, nx, 4, 16, 128), BF16),
        s0b=v((ny, 2, 8, 16, 128), BF16),
        normed=v((128, 512), BF16),
        normed_t=v((ny // 2, 2, 64, 128), BF16),
        uq=v((128, 512), F32),
        uk=v((128, 512), F32),
        nq=v((128, 512), F32),
        nk=v((128, 512), F32),
        kv=v((128, 1024), BF16),
        packed=v((128, 1024), BF16),
        halo=v((224, 1024), BF16),
        qm=v((4, 256, 128), BF16),
        gm=v((4, 256, 128), BF16),
        mask=v((128, 128), F32),
        mask_h=v((224, 128), F32),
        e_l=v((4, 128, 256), F32),
        d_l=v((4, 128, 256), F32),
        p_h=v((4, 224, 256), BF16),
        ds_h=v((4, 224, 256), BF16),
        gsend=v((224, 1024), BF16),
        grecv=v((224, 1024), BF16),
        gkv=v((128, 1024), F32),
        att=v((128, 512), BF16),
        att_t=v((ny // 2, 2, 64, 128), BF16),
        act=v((128, 1536), BF16),
        gn=v((128, 512), F32),
        inv=v((128, 128), F32),
    )
    names = list(scratch)
    count = reduce_count(nx, ny, nz) + 16

    def kernel(x_ref, dy_ref, gain_ref, wqkv_ref, wout_ref, scale_ref, mixed_ref, gin_ref, gqkv_ref, gout_ref, *rest):
        b = dict(zip(names, rest))
        links = Links(*rest[len(names) :])
        p = Place()

        def neighbour(dy_step, dx_step):
            return ((p.gy + dy_step) % p.ngy, (p.gx + dx_step) % p.ngx, p.z)

        arrive = enter(p.reduce_peers() + [neighbour(*block[3:]) for block in BLOCKS])

        def exchange(source, target):
            return [
                links.start(source(start, size), target.at[land : land + size], neighbour(*step))
                for start, size, land, *step in BLOCKS
            ]

        low = iota((128, 128), 1) < 64
        ones = jnp.where((iota((128, 128), 0) < 64) == low, 1.0, 0.0).astype(BF16)

        def masked(a):
            zero = jnp.zeros_like(a)
            return jnp.concatenate([jnp.where(low, a, zero), jnp.where(low, zero, a)], axis=0).astype(BF16)

        xf = x_ref[...].astype(F32)
        inv_rms = lax.rsqrt(jnp.sum(xf * xf, -1, keepdims=True) * (1.0 / 512) + 1e-6)
        b["inv"][...] = jnp.broadcast_to(inv_rms, (128, 128))
        normed_f = xf * inv_rms * gain_ref[...]
        normed = normed_f.astype(BF16)
        b["normed"][...] = normed
        for i in range(4):
            lanes = slice(i * 128, i * 128 + 128)
            k_raw = dot(normed, wqkv_ref[:, 512 + i * 128 : 640 + i * 128])
            nk = lax.rsqrt(head_sum(k_raw * k_raw, ones) + 1e-6)
            uk = k_raw * nk
            b["nk"][:, lanes] = nk
            b["uk"][:, lanes] = uk
            b["kv"][:, lanes] = uk.astype(BF16)
        b["kv"][:, 512:1024] = dot(normed, wqkv_ref[:, 1024:1536]).astype(BF16)
        choose = jnp.where(edge_tokens(iota((128, 128), 0)) == iota((128, 128), 1), 1.0, 0.0)
        b["packed"][...] = dot(choose.astype(BF16), b["kv"][...]).astype(BF16)
        arrive()

        def key_block(start, size):
            if start == 0:
                return b["kv"].at[0:48]
            if start == 48:
                return b["kv"].at[80:128]
            return b["packed"].at[start - 96 : start - 96 + size]

        keys = exchange(key_block, b["halo"])

        for i in range(4):
            lanes = slice(i * 128, i * 128 + 128)
            q_raw = dot(normed, wqkv_ref[:, lanes])
            nq = lax.rsqrt(head_sum(q_raw * q_raw, ones) + 1e-6)
            uq = q_raw * nq
            scale = jnp.where(low, scale_ref[2 * i], scale_ref[2 * i + 1])
            b["nq"][:, lanes] = nq * scale
            b["uq"][:, lanes] = uq
            b["qm"][i] = masked(uq * scale)
            b["gm"][i] = masked(dot(dy_ref[...], wout_ref[lanes, :], TURN))

        token = iota((128, 128), 0)
        b["mask"][...] = jnp.where(near(token >> 4, token & 15, (128, 128)), 1.0, 0.0)
        row, col, there = halo_place(iota((224, 128), 0))
        all_row, all_col = row + p.gy * 8, col + p.gx * 16
        there = there & (all_row >= 0) & (all_row < 8 * p.ngy) & (all_col >= 0) & (all_col < 16 * p.ngx)
        b["mask_h"][...] = jnp.where(there & near(row, col, (224, 128)), 1.0, 0.0)
        sums, mids = [], []
        for i in range(4):
            lanes, more = slice(i * 128, i * 128 + 128), slice(512 + i * 128, 640 + i * 128)
            e = jnp.exp(dot(b["kv"][:, lanes], b["qm"][i], TURN)) * twice(b["mask"][...])
            d = dot(b["kv"][:, more], b["gm"][i], TURN)
            b["e_l"][i] = e
            b["d_l"][i] = d
            sums.append(jnp.sum(e, 0, keepdims=True))
            mids.append(jnp.sum(e * d, 0, keepdims=True))
        for i in range(4):
            lanes = slice(i * 128, i * 128 + 128)
            b["normed_t"][i] = b["normed"][:, lanes].astype(F32).T.astype(BF16).reshape(2, 64, 128)
        for c in keys:
            c.wait_recv()

        for i in range(4):
            lanes, more = slice(i * 128, i * 128 + 128), slice(512 + i * 128, 640 + i * 128)
            e = jnp.exp(dot(b["halo"][:, lanes], b["qm"][i], TURN)) * twice(b["mask_h"][...])
            d = dot(b["halo"][:, more], b["gm"][i], TURN)
            inverse = 1.0 / (sums[i] + jnp.sum(e, 0, keepdims=True))
            mids[i] = (mids[i] + jnp.sum(e * d, 0, keepdims=True)) * inverse
            sums[i] = inverse
            probs = e * inverse
            ds = (probs * (d - mids[i])).astype(BF16)
            probs = probs.astype(BF16)
            b["p_h"][i] = probs
            b["ds_h"][i] = ds
            b["gsend"][:, lanes] = dot(ds, b["qm"][i]).astype(BF16)
            b["gsend"][:, more] = dot(probs, b["gm"][i]).astype(BF16)
        grads = exchange(lambda start, size: b["gsend"].at[start : start + size], b["grecv"])

        for i in range(4):
            lanes, more = slice(i * 128, i * 128 + 128), slice(512 + i * 128, 640 + i * 128)
            probs = b["e_l"][i] * sums[i]
            ds = (probs * (b["d_l"][i] - mids[i])).astype(BF16)
            probs = probs.astype(BF16)
            att_t = pick(dot(b["kv"][:, more], probs, FIRST) + dot(b["halo"][:, more], b["p_h"][i], FIRST))
            gqs_t = pick(dot(b["kv"][:, lanes], ds, FIRST) + dot(b["halo"][:, lanes], b["ds_h"][i], FIRST))
            half = att_t.astype(BF16)
            b["att_t"][i] = half.reshape(2, 64, 128)
            att = att_t.T.astype(BF16)
            b["att"][:, lanes] = att
            gqs = gqs_t.T
            uq = b["uq"][:, lanes]
            grad_q = b["nq"][:, lanes] * (gqs - uq * head_sum(uq * gqs, ones))
            b["act"][:, lanes] = grad_q.astype(BF16)
            b["gkv"][:, lanes] = dot(ds, b["qm"][i])
            b["gkv"][:, more] = dot(probs, b["gm"][i])

        rows = 32 * ny

        def part_a(core):
            left = b["normed_t"][:, core].reshape(rows, 128)
            right = b["att_t"][:, core].reshape(rows, 128)
            q_part = dot(left, b["act"][:, 0:512])
            out_part = dot(right, dy_ref[...])
            return [
                jnp.concatenate(
                    [a[:, t * 128 : t * 128 + 128].reshape(ny, nx, 8, 128) for a in (q_part, out_part)], axis=2
                )
                for t in range(4)
            ]

        for t, tile in enumerate(part_a(1 - p.core)):
            b["s0a"][:, :, t] = tile.astype(BF16)
        first_a = links.start(b["s0a"], b["r0a"], p.other_core())
        for t, tile in enumerate(part_a(p.core)):
            b["own_a"][:, :, t] = tile
        mixed_ref[...] = (x_ref[...].astype(F32) + dot(b["att"][...], wout_ref[...])).astype(BF16)
        b["gn"][...] = dot(b["act"][:, 0:512], wqkv_ref[:, 0:512], TURN)
        xs = start_a(p, links, b, first_a)

        for c in grads:
            c.wait_recv()
        back = jnp.where(edge_tokens(iota((128, 128), 1)) == iota((128, 128), 0), 1.0, 0.0)
        total = b["gkv"][...] + dot(back.astype(BF16), b["grecv"][96:224, :])
        total = jnp.concatenate(
            [
                total[0:48] + b["grecv"][0:48, :].astype(F32),
                total[48:80],
                total[80:128] + b["grecv"][48:96, :].astype(F32),
            ],
            axis=0,
        )
        for i in range(4):
            lanes, more = slice(i * 128, i * 128 + 128), slice(512 + i * 128, 640 + i * 128)
            uk = b["uk"][:, lanes]
            gku = total[:, lanes]
            b["act"][:, more] = (b["nk"][:, lanes] * (gku - uk * head_sum(uk * gku, ones))).astype(BF16)
        b["act"][:, 1024:1536] = total[:, 512:1024].astype(BF16)

        def part_b(core):
            left = b["normed_t"][:, core].reshape(rows, 128)
            a = dot(left, b["act"][:, 512:1536])
            return [a[:, t * 128 : t * 128 + 128].reshape(ny, 2, 16, 128) for t in range(8)]

        for t, tile in enumerate(part_b(1 - p.core)):
            b["s0b"][:, :, t] = tile.astype(BF16)
        first_b = links.start(b["s0b"], b["r0b"], p.other_core())
        for t, tile in enumerate(part_b(p.core)):
            b["own_b"][:, :, t] = tile

        def finish():
            grad_n = b["gn"][...] + dot(b["act"][:, 512:1536], wqkv_ref[:, 512:1536], TURN)
            g = grad_n * gain_ref[...]
            xf = x_ref[...].astype(F32)
            inv = b["inv"][:, 0:1]
            mean = jnp.sum(xf * g, -1, keepdims=True) * (1.0 / 512)
            gin_ref[...] = (dy_ref[...].astype(F32) + inv * g - xf * (inv * inv * inv * mean)).astype(BF16)

        reduce_tail(p, links, b, first_b, xs, finish, factor)
        write_rows(b, gqkv_ref, gout_ref)
        links.drain()

    vm = pl.BlockSpec(memory_space=pltpu.VMEM)
    return pl.pallas_call(
        kernel,
        out_shape=(
            jax.ShapeDtypeStruct((128, 512), BF16),
            jax.ShapeDtypeStruct((128, 512), BF16),
            jax.ShapeDtypeStruct((8, 1536), F32),
            jax.ShapeDtypeStruct((8, 512), F32),
        ),
        in_specs=[vm] * 5 + [pl.BlockSpec(memory_space=pltpu.SMEM)],
        out_specs=(vm, vm, vm, vm),
        scratch_shapes=[scratch[n] for n in names]
        + [pltpu.SemaphoreType.DMA((count,)), pltpu.SemaphoreType.DMA((count,))],
        compiler_params=pltpu.CompilerParams(
            collective_id=1, has_side_effects=True, vmem_limit_bytes=56 * 1024 * 1024
        ),
        cost_estimate=pl.CostEstimate(flops=10**9, bytes_accessed=4 * 10**6, transcendentals=10**6),
        name="block",
    )(x, dy, gain, w_qkv, w_out, head_scale)


def per_device(inputs, cotangent, norm_gain, w_qkv, w_out, head_scale):
    shape, width = inputs.shape, inputs.shape[-1]
    tokens = shape[1] * shape[2]
    factor = 1.0 / math.sqrt(
        lax.axis_size("img") * lax.axis_size("gy") * lax.axis_size("gx") * tokens
    )
    mixed, grad_input, grad_qkv, grad_out = block_call(
        inputs.reshape(tokens, width),
        cotangent.reshape(tokens, width),
        norm_gain.reshape(1, width),
        w_qkv,
        w_out,
        head_scale,
        factor,
    )
    return (mixed.reshape(shape), grad_input.reshape(shape), grad_qkv, grad_out)


def solution(mesh):
    tokens, rows = P("img", "gy", "gx", None), P(("gy", "gx"), None)
    return jax.shard_map(
        per_device,
        mesh=mesh,
        in_specs=(tokens, tokens, P(), P(), P(), P()),
        out_specs=(tokens, tokens, rows, rows),
        check_vma=False,
    )
```

time: 175 us -> 67.1 us (0.38)
  the two profiles are of different devices: /device:TPU:6 before, /device:TPU:8 now
where the time goes in v2:
time: 67.1 us; the launch traced here: 66.8 us
  Pallas kernels  60.3 us (90%)
  local copies, waits for them, and re-layouts  5.88 us (9%)
    pallas_call x1, Pallas kernels, block_call(): pl.pallas_call(kernel, out_shape=(jax.ShapeDtypeStruct((128, 512), BF16),...  60.3 us
    unnamed x4, local copies, waits for them, and re-layouts  5.88 us

profile of v2, /device:TPU:8, one launch (start us, length us, event | category | flops | bytes accessed | tf_op | source)
XLA Modules:
  0.0 66.8 jit_solution(6938156896878064054)
XLA Ops:
  0.6 60.3 %block.1 = (bf16[128,512]{1,0:T(8,128)(2,1)}, bf16[128,512]{1,0:T(8,128)(2,1)}, f32[8,1536]{1,0:T(8,128)}, f32[8,512]{1,0:T(8,128)}) custom-call(bf16[128,512]{1,0:T(8,128)(2,1)} %bitcast.7, bf16[128,512]{1,0:T(8,128)(2,1)} %bitcast.8, f32[1,512]{1,0:T(1,128)} %bitcast.9, bf16[512,1536]{1,0:T(8,128)(2,1)} %wqkv_ref.1, bf16[512,512]{1,0:T(8,128)(2,1)} %wout_ref.1, ...), custom_call_target="tpu_custom_call" | custom-call | flops 1000000000 | bytes 4000000 | tf_op jit(solution)/shard_map/block/pallas_call | solution.py:540
  60.9 1.6 %copy.14 = bf16[1,8,16,512]{3,2,1,0:T(8,128)(2,1)} copy(bf16[1,8,16,512]{3,2,1,0:T(8,128)(2,1)} %bitcast.6) | data formatting | bytes 262144
  62.5 1.6 %copy.15 = bf16[1,8,16,512]{3,2,1,0:T(8,128)(2,1)} copy(bf16[1,8,16,512]{3,2,1,0:T(8,128)(2,1)} %bitcast.5) | data formatting | bytes 262144
  64.0 1.4 %copy.16 = f32[8,1536]{1,0:T(8,128)} copy(f32[8,1536]{1,0:T(8,128)} %get-tuple-element.18) | data formatting | bytes 98304
  65.5 1.3 %copy.17 = f32[8,512]{1,0:T(8,128)} copy(f32[8,512]{1,0:T(8,128)} %get-tuple-element.19) | data formatting | bytes 32768

commit v3 on v2

--- a/solution.py
+++ b/solution.py
@@ -84,9 +84,7 @@
         rxa=v((nx - 1, ny, 4, 16, 128), BF16),
         s2a=v((ny, 4, 16, 128), BF16),
         rya=v((ny - 1, 4, 16, 128), BF16),
-        ta=v((nz, 8, 128), F32),
-        rza=v((nz - 1, 8, 128), F32),
-        ga=v((nz, 8, 128), F32),
+        za=v((nz, 4, 16, 128), BF16),
         ryb=v((ny - 1, 8, 16, 128), BF16),
         rzb=v((nz - 1, ny, 16, 128), BF16),
         syb=v((nz, 16, 128), BF16),
@@ -100,7 +98,7 @@
 
 
 def reduce_count(nx, ny, nz):
-    return 2 + 2 * (nx - 1) + 3 * (ny - 1) + 5 * (nz - 1)
+    return 2 + 2 * (nx - 1) + 3 * (ny - 1) + 4 * (nz - 1)
 
 
 def core_add(s1, own, got):
@@ -121,7 +119,7 @@
     return xs
 
 
-def reduce_tail(p, links, b, first_b, xs, finish, factor):
+def reduce_tail(p, links, b, first_b, xs, send_grads, finish, factor, qkv_ref, out_ref):
     nx, ny, nz = p.nx, p.ny, p.nz
     first_b.wait_recv()
     core_add(b["s1b"], b["own_b"], b["r0b"])
@@ -133,7 +131,7 @@
         if k < nz:
             to, device = p.z_peer(k)
             zs.append(links.start(b["s1b"].at[:, 1, to], b["rzb"].at[k - 1], device))
-    finish()
+    send_grads()
 
     for c in xs:
         c.wait_recv()
@@ -188,12 +186,11 @@
     total = b["s2a"][p.y].astype(F32)
     for k in range(ny - 1):
         total += b["rya"][k].astype(F32)
-    b["ta"][0:4] = total[:, 0:8]
-    b["ta"][4:8] = total[:, 8:16]
-    z2 = []
+    b["za"][p.z] = total.astype(BF16)
+    last_a = []
     for k in range(1, nz):
         to, device = p.z_peer(k)
-        z2.append(links.start(b["ta"].at[to], b["rza"].at[k - 1], device))
+        last_a.append(links.start(b["za"].at[p.z], b["za"].at[p.z], device))
 
     for c in z3:
         c.wait_recv()
@@ -214,35 +211,28 @@
         to, device = p.x_peer(k)
         x3.append(links.start(b["ub"].at[to], b["r3x"].at[k - 1], device))
 
-    for c in z2:
-        c.wait_recv()
-    total = b["ta"][p.z]
-    for k in range(nz - 1):
-        total += b["rza"][k]
-    b["ga"][p.z] = total * factor
-    last = []
-    for k in range(1, nz):
-        to, device = p.z_peer(k)
-        last.append(links.start(b["ga"].at[p.z], b["ga"].at[p.z], device))
-
+    finish()
     for c in x3:
         c.wait_recv()
     total = b["ub"][p.x]
     for k in range(nx - 1):
         total += b["r3x"][k]
     b["gb"][p.z] = total * factor
+    last = []
     for k in range(1, nz):
         to, device = p.z_peer(k)
         last.append(links.start(b["gb"].at[p.z], b["gb"].at[p.z], device))
+    for c in last_a:
+        c.wait_recv()
+    total = b["za"][0].astype(F32)
+    for z in range(1, nz):
+        total += b["za"][z].astype(F32)
+    total = total * factor
+    for t in range(4):
+        qkv_ref[:, t * 128 : t * 128 + 128] = total[t, 0:8]
+        out_ref[:, t * 128 : t * 128 + 128] = total[t, 8:16]
     for c in last:
         c.wait_recv()
-
-
-def write_rows(b, qkv_ref, out_ref):
-    for t in range(4):
-        lanes = slice(t * 128, t * 128 + 128)
-        qkv_ref[:, lanes] = b["ga"][t]
-        out_ref[:, lanes] = b["ga"][4 + t]
     for t in range(8):
         qkv_ref[:, 512 + t * 128 : 640 + t * 128] = b["gb"][t]
 
@@ -326,14 +316,24 @@
         s0a=v((ny, nx, 4, 16, 128), BF16),
         s0b=v((ny, 2, 8, 16, 128), BF16),
         normed=v((128, 512), BF16),
+        normed_h=v((224, 512), BF16),
         normed_t=v((ny // 2, 2, 64, 128), BF16),
         uq=v((128, 512), F32),
         uk=v((128, 512), F32),
         nq=v((128, 512), F32),
         nk=v((128, 512), F32),
+        x=v((128, 512), BF16),
+        dy=v((128, 512), BF16),
+        wqkv=v((512, 1536), BF16),
+        wout=v((512, 512), BF16),
         kv=v((128, 1024), BF16),
-        packed=v((128, 1024), BF16),
+        packed=v((128, 512), BF16),
+        halo_x=v((224, 512), BF16),
         halo=v((224, 1024), BF16),
+        uk_h=v((224, 512), F32),
+        nk_h=v((224, 512), F32),
+        normed_th=v((ny // 2, 2, 64, 224), BF16),
+        act_h=v((224, 1024), BF16),
         qm=v((4, 256, 128), BF16),
         gm=v((4, 256, 128), BF16),
         mask=v((128, 128), F32),
@@ -341,22 +341,32 @@
         e_l=v((4, 128, 256), F32),
         d_l=v((4, 128, 256), F32),
         p_h=v((4, 224, 256), BF16),
+        p_l=v((4, 128, 256), BF16),
+        ds_l=v((4, 128, 256), BF16),
         ds_h=v((4, 224, 256), BF16),
-        gsend=v((224, 1024), BF16),
-        grecv=v((224, 1024), BF16),
-        gkv=v((128, 1024), F32),
+        gsend=v((224, 512), BF16),
+        grecv=v((224, 512), BF16),
         att=v((128, 512), BF16),
         att_t=v((ny // 2, 2, 64, 128), BF16),
         act=v((128, 1536), BF16),
-        gn=v((128, 512), F32),
         inv=v((128, 128), F32),
     )
     names = list(scratch)
     count = reduce_count(nx, ny, nz) + 16
 
-    def kernel(x_ref, dy_ref, gain_ref, wqkv_ref, wout_ref, scale_ref, mixed_ref, gin_ref, gqkv_ref, gout_ref, *rest):
+    def kernel(x_hbm, dy_hbm, gain_ref, wqkv_hbm, wout_hbm, scale_ref, mixed_ref, gin_ref, gqkv_ref, gout_ref, *rest):
         b = dict(zip(names, rest))
-        links = Links(*rest[len(names) :])
+        links = Links(*rest[len(names) : len(names) + 2])
+        load_sem = rest[-1]
+        x_ref, dy_ref, wqkv_ref, wout_ref = b["x"], b["dy"], b["wqkv"], b["wout"]
+        loads = [
+            pltpu.make_async_copy(source, target, load_sem.at[i])
+            for i, (source, target) in enumerate(
+                ((x_hbm, x_ref), (wqkv_hbm, wqkv_ref), (dy_hbm, dy_ref), (wout_hbm, wout_ref))
+            )
+        ]
+        for c in loads:
+            c.start()
         p = Place()
 
         def neighbour(dy_step, dx_step):
@@ -377,37 +387,57 @@
             zero = jnp.zeros_like(a)
             return jnp.concatenate([jnp.where(low, a, zero), jnp.where(low, zero, a)], axis=0).astype(BF16)
 
-        xf = x_ref[...].astype(F32)
-        inv_rms = lax.rsqrt(jnp.sum(xf * xf, -1, keepdims=True) * (1.0 / 512) + 1e-6)
+        choose = jnp.where(edge_tokens(iota((128, 128), 0)) == iota((128, 128), 1), 1.0, 0.0)
+        loads[0].wait()
+        b["packed"][...] = dot(choose.astype(BF16), x_ref[...]).astype(BF16)
+        arrive()
+
+        def edge_block(start, size):
+            if start == 0:
+                return x_ref.at[0:48]
+            if start == 48:
+                return x_ref.at[80:128]
+            return b["packed"].at[start - 96 : start - 96 + size]
+
+        edges = exchange(edge_block, b["halo_x"])
+
+        def norm(source, normed_ref, turned_ref):
+            xf = source[...].astype(F32)
+            inv_rms = lax.rsqrt(jnp.sum(xf * xf, -1, keepdims=True) * (1.0 / 512) + 1e-6)
+            normed = xf * inv_rms * gain_ref[...]
+            normed_ref[...] = normed.astype(BF16)
+            for i in range(4):
+                turned = normed[:, i * 128 : i * 128 + 128].T.astype(BF16)
+                turned_ref[i] = turned.reshape(2, 64, turned.shape[1])
+            return inv_rms
+
+        def keys_values(normed_ref, uk_ref, nk_ref, kv_ref):
+            normed = normed_ref[...]
+            for i in range(4):
+                lanes = slice(i * 128, i * 128 + 128)
+                k_raw = dot(normed, wqkv_ref[:, 512 + i * 128 : 640 + i * 128])
+                nk = lax.rsqrt(head_sum(k_raw * k_raw, ones) + 1e-6)
+                uk = k_raw * nk
+                nk_ref[:, lanes] = nk
+                uk_ref[:, lanes] = uk
+                kv_ref[:, lanes] = uk.astype(BF16)
+            kv_ref[:, 512:1024] = dot(normed, wqkv_ref[:, 1024:1536]).astype(BF16)
+
+        inv_rms = norm(x_ref, b["normed"], b["normed_t"])
         b["inv"][...] = jnp.broadcast_to(inv_rms, (128, 128))
-        normed_f = xf * inv_rms * gain_ref[...]
-        normed = normed_f.astype(BF16)
-        b["normed"][...] = normed
+        token = iota((128, 128), 0)
+        b["mask"][...] = jnp.where(near(token >> 4, token & 15, (128, 128)), 1.0, 0.0)
+        row, col, there = halo_place(iota((224, 128), 0))
+        all_row, all_col = row + p.gy * 8, col + p.gx * 16
+        there = there & (all_row >= 0) & (all_row < 8 * p.ngy) & (all_col >= 0) & (all_col < 16 * p.ngx)
+        b["mask_h"][...] = jnp.where(there & near(row, col, (224, 128)), 1.0, 0.0)
+        loads[1].wait()
+        keys_values(b["normed"], b["uk"], b["nk"], b["kv"])
+        loads[2].wait()
+        loads[3].wait()
         for i in range(4):
             lanes = slice(i * 128, i * 128 + 128)
-            k_raw = dot(normed, wqkv_ref[:, 512 + i * 128 : 640 + i * 128])
-            nk = lax.rsqrt(head_sum(k_raw * k_raw, ones) + 1e-6)
-            uk = k_raw * nk
-            b["nk"][:, lanes] = nk
-            b["uk"][:, lanes] = uk
-            b["kv"][:, lanes] = uk.astype(BF16)
-        b["kv"][:, 512:1024] = dot(normed, wqkv_ref[:, 1024:1536]).astype(BF16)
-        choose = jnp.where(edge_tokens(iota((128, 128), 0)) == iota((128, 128), 1), 1.0, 0.0)
-        b["packed"][...] = dot(choose.astype(BF16), b["kv"][...]).astype(BF16)
-        arrive()
-
-        def key_block(start, size):
-            if start == 0:
-                return b["kv"].at[0:48]
-            if start == 48:
-                return b["kv"].at[80:128]
-            return b["packed"].at[start - 96 : start - 96 + size]
-
-        keys = exchange(key_block, b["halo"])
-
-        for i in range(4):
-            lanes = slice(i * 128, i * 128 + 128)
-            q_raw = dot(normed, wqkv_ref[:, lanes])
+            q_raw = dot(b["normed"][...], wqkv_ref[:, lanes])
             nq = lax.rsqrt(head_sum(q_raw * q_raw, ones) + 1e-6)
             uq = q_raw * nq
             scale = jnp.where(low, scale_ref[2 * i], scale_ref[2 * i + 1])
@@ -416,12 +446,6 @@
             b["qm"][i] = masked(uq * scale)
             b["gm"][i] = masked(dot(dy_ref[...], wout_ref[lanes, :], TURN))
 
-        token = iota((128, 128), 0)
-        b["mask"][...] = jnp.where(near(token >> 4, token & 15, (128, 128)), 1.0, 0.0)
-        row, col, there = halo_place(iota((224, 128), 0))
-        all_row, all_col = row + p.gy * 8, col + p.gx * 16
-        there = there & (all_row >= 0) & (all_row < 8 * p.ngy) & (all_col >= 0) & (all_col < 16 * p.ngx)
-        b["mask_h"][...] = jnp.where(there & near(row, col, (224, 128)), 1.0, 0.0)
         sums, mids = [], []
         for i in range(4):
             lanes, more = slice(i * 128, i * 128 + 128), slice(512 + i * 128, 640 + i * 128)
@@ -431,53 +455,44 @@
             b["d_l"][i] = d
             sums.append(jnp.sum(e, 0, keepdims=True))
             mids.append(jnp.sum(e * d, 0, keepdims=True))
-        for i in range(4):
-            lanes = slice(i * 128, i * 128 + 128)
-            b["normed_t"][i] = b["normed"][:, lanes].astype(F32).T.astype(BF16).reshape(2, 64, 128)
-        for c in keys:
+        for c in edges:
             c.wait_recv()
+
+        norm(b["halo_x"], b["normed_h"], b["normed_th"])
+        keys_values(b["normed_h"], b["uk_h"], b["nk_h"], b["halo"])
+
+        def key_gradient(uk, nk, gku):
+            return (nk * (gku - uk * head_sum(uk * gku, ones))).astype(BF16)
 
         for i in range(4):
             lanes, more = slice(i * 128, i * 128 + 128), slice(512 + i * 128, 640 + i * 128)
             e = jnp.exp(dot(b["halo"][:, lanes], b["qm"][i], TURN)) * twice(b["mask_h"][...])
             d = dot(b["halo"][:, more], b["gm"][i], TURN)
             inverse = 1.0 / (sums[i] + jnp.sum(e, 0, keepdims=True))
-            mids[i] = (mids[i] + jnp.sum(e * d, 0, keepdims=True)) * inverse
-            sums[i] = inverse
-            probs = e * inverse
-            ds = (probs * (d - mids[i])).astype(BF16)
+            mid = (mids[i] + jnp.sum(e * d, 0, keepdims=True)) * inverse
+            probs_h = e * inverse
+            ds_h = (probs_h * (d - mid)).astype(BF16)
+            probs_h = probs_h.astype(BF16)
+            probs = b["e_l"][i] * inverse
+            ds = (probs * (b["d_l"][i] - mid)).astype(BF16)
             probs = probs.astype(BF16)
-            b["p_h"][i] = probs
-            b["ds_h"][i] = ds
-            b["gsend"][:, lanes] = dot(ds, b["qm"][i]).astype(BF16)
-            b["gsend"][:, more] = dot(probs, b["gm"][i]).astype(BF16)
-        grads = exchange(lambda start, size: b["gsend"].at[start : start + size], b["grecv"])
-
-        for i in range(4):
-            lanes, more = slice(i * 128, i * 128 + 128), slice(512 + i * 128, 640 + i * 128)
-            probs = b["e_l"][i] * sums[i]
-            ds = (probs * (b["d_l"][i] - mids[i])).astype(BF16)
-            probs = probs.astype(BF16)
-            att_t = pick(dot(b["kv"][:, more], probs, FIRST) + dot(b["halo"][:, more], b["p_h"][i], FIRST))
-            gqs_t = pick(dot(b["kv"][:, lanes], ds, FIRST) + dot(b["halo"][:, lanes], b["ds_h"][i], FIRST))
-            half = att_t.astype(BF16)
-            b["att_t"][i] = half.reshape(2, 64, 128)
-            att = att_t.T.astype(BF16)
-            b["att"][:, lanes] = att
+            b["p_h"][i] = probs_h
+            b["ds_h"][i] = ds_h
+            b["p_l"][i] = probs
+            b["ds_l"][i] = ds
+            att_t = pick(dot(b["kv"][:, more], probs, FIRST) + dot(b["halo"][:, more], probs_h, FIRST))
+            gqs_t = pick(dot(b["kv"][:, lanes], ds, FIRST) + dot(b["halo"][:, lanes], ds_h, FIRST))
+            b["att_t"][i] = att_t.astype(BF16).reshape(2, 64, 128)
+            b["att"][:, lanes] = att_t.T.astype(BF16)
             gqs = gqs_t.T
             uq = b["uq"][:, lanes]
-            grad_q = b["nq"][:, lanes] * (gqs - uq * head_sum(uq * gqs, ones))
-            b["act"][:, lanes] = grad_q.astype(BF16)
-            b["gkv"][:, lanes] = dot(ds, b["qm"][i])
-            b["gkv"][:, more] = dot(probs, b["gm"][i])
+            b["act"][:, lanes] = (b["nq"][:, lanes] * (gqs - uq * head_sum(uq * gqs, ones))).astype(BF16)
 
         rows = 32 * ny
 
         def part_a(core):
-            left = b["normed_t"][:, core].reshape(rows, 128)
-            right = b["att_t"][:, core].reshape(rows, 128)
-            q_part = dot(left, b["act"][:, 0:512])
-            out_part = dot(right, dy_ref[...])
+            q_part = dot(b["normed_t"][:, core].reshape(rows, 128), b["act"][:, 0:512])
+            out_part = dot(b["att_t"][:, core].reshape(rows, 128), dy_ref[...])
             return [
                 jnp.concatenate(
                     [a[:, t * 128 : t * 128 + 128].reshape(ny, nx, 8, 128) for a in (q_part, out_part)], axis=2
@@ -490,53 +505,56 @@
         first_a = links.start(b["s0a"], b["r0a"], p.other_core())
         for t, tile in enumerate(part_a(p.core)):
             b["own_a"][:, :, t] = tile
-        mixed_ref[...] = (x_ref[...].astype(F32) + dot(b["att"][...], wout_ref[...])).astype(BF16)
-        b["gn"][...] = dot(b["act"][:, 0:512], wqkv_ref[:, 0:512], TURN)
-        xs = start_a(p, links, b, first_a)
-
-        for c in grads:
-            c.wait_recv()
-        back = jnp.where(edge_tokens(iota((128, 128), 1)) == iota((128, 128), 0), 1.0, 0.0)
-        total = b["gkv"][...] + dot(back.astype(BF16), b["grecv"][96:224, :])
-        total = jnp.concatenate(
-            [
-                total[0:48] + b["grecv"][0:48, :].astype(F32),
-                total[48:80],
-                total[80:128] + b["grecv"][48:96, :].astype(F32),
-            ],
-            axis=0,
-        )
+
         for i in range(4):
             lanes, more = slice(i * 128, i * 128 + 128), slice(512 + i * 128, 640 + i * 128)
-            uk = b["uk"][:, lanes]
-            gku = total[:, lanes]
-            b["act"][:, more] = (b["nk"][:, lanes] * (gku - uk * head_sum(uk * gku, ones))).astype(BF16)
-        b["act"][:, 1024:1536] = total[:, 512:1024].astype(BF16)
+            b["act_h"][:, lanes] = key_gradient(b["uk_h"][:, lanes], b["nk_h"][:, lanes], dot(b["ds_h"][i], b["qm"][i]))
+            b["act_h"][:, more] = dot(b["p_h"][i], b["gm"][i]).astype(BF16)
+            b["act"][:, more] = key_gradient(b["uk"][:, lanes], b["nk"][:, lanes], dot(b["ds_l"][i], b["qm"][i]))
+            b["act"][:, 1024 + i * 128 : 1152 + i * 128] = dot(b["p_l"][i], b["gm"][i]).astype(BF16)
 
         def part_b(core):
-            left = b["normed_t"][:, core].reshape(rows, 128)
-            a = dot(left, b["act"][:, 512:1536])
+            a = dot(b["normed_t"][:, core].reshape(rows, 128), b["act"][:, 512:1536])
+            a += dot(b["normed_th"][:, core].reshape(rows, 224), b["act_h"][...])
             return [a[:, t * 128 : t * 128 + 128].reshape(ny, 2, 16, 128) for t in range(8)]
 
+        xs = start_a(p, links, b, first_a)
         for t, tile in enumerate(part_b(1 - p.core)):
             b["s0b"][:, :, t] = tile.astype(BF16)
         first_b = links.start(b["s0b"], b["r0b"], p.other_core())
         for t, tile in enumerate(part_b(p.core)):
             b["own_b"][:, :, t] = tile
+        b["gsend"][...] = dot(b["act_h"][...], wqkv_ref[:, 512:1536], TURN).astype(BF16)
+        grads = []
+
+        def send_grads():
+            grads.extend(exchange(lambda start, size: b["gsend"].at[start : start + size], b["grecv"]))
+            mixed_ref[...] = (x_ref[...].astype(F32) + dot(b["att"][...], wout_ref[...])).astype(BF16)
 
         def finish():
-            grad_n = b["gn"][...] + dot(b["act"][:, 512:1536], wqkv_ref[:, 512:1536], TURN)
+            grad_n = dot(b["act"][...], wqkv_ref[...], TURN)
+            back = jnp.where(edge_tokens(iota((128, 128), 1)) == iota((128, 128), 0), 1.0, 0.0)
+            for c in grads:
+                c.wait_recv()
+            grad_n += dot(back.astype(BF16), b["grecv"][96:224, :])
+            grad_n = jnp.concatenate(
+                [
+                    grad_n[0:48] + b["grecv"][0:48, :].astype(F32),
+                    grad_n[48:80],
+                    grad_n[80:128] + b["grecv"][48:96, :].astype(F32),
+                ],
+                axis=0,
+            )
             g = grad_n * gain_ref[...]
             xf = x_ref[...].astype(F32)
             inv = b["inv"][:, 0:1]
             mean = jnp.sum(xf * g, -1, keepdims=True) * (1.0 / 512)
             gin_ref[...] = (dy_ref[...].astype(F32) + inv * g - xf * (inv * inv * inv * mean)).astype(BF16)
 
-        reduce_tail(p, links, b, first_b, xs, finish, factor)
-        write_rows(b, gqkv_ref, gout_ref)
+        reduce_tail(p, links, b, first_b, xs, send_grads, finish, factor, gqkv_ref, gout_ref)
         links.drain()
 
-    vm = pl.BlockSpec(memory_space=pltpu.VMEM)
+    vm, anywhere = pl.BlockSpec(memory_space=pltpu.VMEM), pl.BlockSpec(memory_space=pl.ANY)
     return pl.pallas_call(
         kernel,
         out_shape=(
@@ -545,10 +563,10 @@
             jax.ShapeDtypeStruct((8, 1536), F32),
             jax.ShapeDtypeStruct((8, 512), F32),
         ),
-        in_specs=[vm] * 5 + [pl.BlockSpec(memory_space=pltpu.SMEM)],
+        in_specs=[anywhere, anywhere, vm, anywhere, anywhere, pl.BlockSpec(memory_space=pltpu.SMEM)],
         out_specs=(vm, vm, vm, vm),
         scratch_shapes=[scratch[n] for n in names]
-        + [pltpu.SemaphoreType.DMA((count,)), pltpu.SemaphoreType.DMA((count,))],
+        + [pltpu.SemaphoreType.DMA((count,)), pltpu.SemaphoreType.DMA((count,)), pltpu.SemaphoreType.DMA((4,))],
         compiler_params=pltpu.CompilerParams(
             collective_id=1, has_side_effects=True, vmem_limit_bytes=56 * 1024 * 1024
         ),
@@ -557,13 +575,30 @@
     )(x, dy, gain, w_qkv, w_out, head_scale)
 
 
+def hand_over(*arrays):
+    count = len(arrays)
+
+    def kernel(*refs):
+        for i in range(count):
+            refs[count + i][...] = refs[i][...]
+
+    vm = pl.BlockSpec(memory_space=pltpu.VMEM)
+    return pl.pallas_call(
+        kernel,
+        out_shape=tuple(jax.ShapeDtypeStruct(a.shape, a.dtype) for a in arrays),
+        in_specs=[vm] * count,
+        out_specs=(vm,) * count,
+        name="hand_over",
+    )(*arrays)
+
+
 def per_device(inputs, cotangent, norm_gain, w_qkv, w_out, head_scale):
     shape, width = inputs.shape, inputs.shape[-1]
     tokens = shape[1] * shape[2]
     factor = 1.0 / math.sqrt(
         lax.axis_size("img") * lax.axis_size("gy") * lax.axis_size("gx") * tokens
     )
-    mixed, grad_input, grad_qkv, grad_out = block_call(
+    results = block_call(
         inputs.reshape(tokens, width),
         cotangent.reshape(tokens, width),
         norm_gain.reshape(1, width),
@@ -572,6 +607,7 @@
         head_scale,
         factor,
     )
+    mixed, grad_input, grad_qkv, grad_out = hand_over(*results)
     return (mixed.reshape(shape), grad_input.reshape(shape), grad_qkv, grad_out)
 
 

time: 67.1 us -> 56.3 us (0.84)
  the two profiles are of different devices: /device:TPU:8 before, /device:TPU:6 now
where the time goes in v3:
time: 56.3 us; the launch traced here: 55.4 us
  Pallas kernels  54.7 us (97%)
  between operations  0.64 us (1%)
    pallas_call x1, Pallas kernels, block_call(): pl.pallas_call(kernel, out_shape=(jax.ShapeDtypeStruct((128, 512), BF16),...  53 us
    pallas_call x1, Pallas kernels, hand_over(): pl.pallas_call(kernel, out_shape=tuple((jax.ShapeDtypeStruct(a.shape, a.d...  1.69 us

profile of v3, /device:TPU:6, one launch (start us, length us, event | category | flops | bytes accessed | tf_op | source)
XLA Modules:
  0.0 55.4 jit_solution(2889265508360599817)
XLA Ops:
  0.6 53.0 %block.1 = (bf16[128,512]{1,0:T(8,128)(2,1)}, bf16[128,512]{1,0:T(8,128)(2,1)}, f32[8,1536]{1,0:T(8,128)}, f32[8,512]{1,0:T(8,128)}) custom-call(bf16[128,512]{1,0:T(8,128)(2,1)} %bitcast.5, bf16[128,512]{1,0:T(8,128)(2,1)} %bitcast.6, f32[1,512]{1,0:T(1,128)} %bitcast.9, bf16[512,1536]{1,0:T(8,128)(2,1)} %wqkv_hbm.1, bf16[512,512]{1,0:T(8,128)(2,1)} %wout_hbm.1, ...), custom_call_target="tpu_custom_call" | custom-call | flops 1000000000 | bytes 4000000 | tf_op jit(solution)/shard_map/block/pallas_call | solution.py:558
  53.7 1.7 %hand_over.1 = (bf16[128,512]{1,0:T(8,128)(2,1)}, bf16[128,512]{1,0:T(8,128)(2,1)}, f32[8,1536]{1,0:T(8,128)}, f32[8,512]{1,0:T(8,128)}) custom-call(bf16[128,512]{1,0:T(8,128)(2,1)} %get-tuple-element.12.refs_0_, bf16[128,512]{1,0:T(8,128)(2,1)} %get-tuple-element.13.refs_1_, f32[8,1536]{1,0:T(8,128)} %get-tuple-element.14.refs_2_, ...), custom_call_target="tpu_custom_call" | custom-call | tf_op jit(solution)/shard_map/hand_over/pallas_call | solution.py:586

commit v4 on v3

--- a/solution.py
+++ b/solution.py
@@ -119,7 +119,7 @@
     return xs
 
 
-def reduce_tail(p, links, b, first_b, xs, send_grads, finish, factor, qkv_ref, out_ref):
+def reduce_tail(p, links, b, first_b, xs, meanwhile, send_grads, finish, factor, qkv_ref, out_ref):
     nx, ny, nz = p.nx, p.ny, p.nz
     first_b.wait_recv()
     core_add(b["s1b"], b["own_b"], b["r0b"])
@@ -131,7 +131,7 @@
         if k < nz:
             to, device = p.z_peer(k)
             zs.append(links.start(b["s1b"].at[:, 1, to], b["rzb"].at[k - 1], device))
-    send_grads()
+    meanwhile()
 
     for c in xs:
         c.wait_recv()
@@ -180,6 +180,7 @@
     for k in range(1, ny):
         to, device = p.y_peer(k)
         y3.append(links.start(b["szb"].at[to], b["r2y"].at[k - 1], device))
+    send_grads()
 
     for c in y2:
         c.wait_recv()
@@ -211,7 +212,6 @@
         to, device = p.x_peer(k)
         x3.append(links.start(b["ub"].at[to], b["r3x"].at[k - 1], device))
 
-    finish()
     for c in x3:
         c.wait_recv()
     total = b["ub"][p.x]
@@ -222,6 +222,7 @@
     for k in range(1, nz):
         to, device = p.z_peer(k)
         last.append(links.start(b["gb"].at[p.z], b["gb"].at[p.z], device))
+    finish()
     for c in last_a:
         c.wait_recv()
     total = b["za"][0].astype(F32)
@@ -345,6 +346,7 @@
         ds_l=v((4, 128, 256), BF16),
         ds_h=v((4, 224, 256), BF16),
         gsend=v((224, 512), BF16),
+        gn=v((128, 512), F32),
         grecv=v((224, 512), BF16),
         att=v((128, 512), BF16),
         att_t=v((ny // 2, 2, 64, 128), BF16),
@@ -524,19 +526,21 @@
         first_b = links.start(b["s0b"], b["r0b"], p.other_core())
         for t, tile in enumerate(part_b(p.core)):
             b["own_b"][:, :, t] = tile
-        b["gsend"][...] = dot(b["act_h"][...], wqkv_ref[:, 512:1536], TURN).astype(BF16)
         grads = []
 
         def send_grads():
             grads.extend(exchange(lambda start, size: b["gsend"].at[start : start + size], b["grecv"]))
+
+        def meanwhile():
+            b["gsend"][...] = dot(b["act_h"][...], wqkv_ref[:, 512:1536], TURN).astype(BF16)
+            b["gn"][...] = dot(b["act"][...], wqkv_ref[...], TURN)
             mixed_ref[...] = (x_ref[...].astype(F32) + dot(b["att"][...], wout_ref[...])).astype(BF16)
 
         def finish():
-            grad_n = dot(b["act"][...], wqkv_ref[...], TURN)
             back = jnp.where(edge_tokens(iota((128, 128), 1)) == iota((128, 128), 0), 1.0, 0.0)
             for c in grads:
                 c.wait_recv()
-            grad_n += dot(back.astype(BF16), b["grecv"][96:224, :])
+            grad_n = b["gn"][...] + dot(back.astype(BF16), b["grecv"][96:224, :])
             grad_n = jnp.concatenate(
                 [
                     grad_n[0:48] + b["grecv"][0:48, :].astype(F32),
@@ -551,7 +555,7 @@
             mean = jnp.sum(xf * g, -1, keepdims=True) * (1.0 / 512)
             gin_ref[...] = (dy_ref[...].astype(F32) + inv * g - xf * (inv * inv * inv * mean)).astype(BF16)
 
-        reduce_tail(p, links, b, first_b, xs, send_grads, finish, factor, gqkv_ref, gout_ref)
+        reduce_tail(p, links, b, first_b, xs, meanwhile, send_grads, finish, factor, gqkv_ref, gout_ref)
         links.drain()
 
     vm, anywhere = pl.BlockSpec(memory_space=pltpu.VMEM), pl.BlockSpec(memory_space=pl.ANY)

time: 56.3 us -> 55.9 us (level)
  no operation moved by 1% of the time
where the time goes in v4:
time: 55.9 us; the launch traced here: 55.4 us
  Pallas kernels  54.8 us (98%)
  between operations  0.64 us (1%)
    pallas_call x1, Pallas kernels, block_call(): pl.pallas_call(kernel, out_shape=(jax.ShapeDtypeStruct((128, 512), BF16),...  53.1 us
    pallas_call x1, Pallas kernels, hand_over(): pl.pallas_call(kernel, out_shape=tuple((jax.ShapeDtypeStruct(a.shape, a.d...  1.69 us

profile of v4, /device:TPU:6, one launch (start us, length us, event | category | flops | bytes accessed | tf_op | source)
XLA Modules:
  0.0 55.4 jit_solution(12944531268983544197)
XLA Ops:
  0.6 53.1 %block.1 = (bf16[128,512]{1,0:T(8,128)(2,1)}, bf16[128,512]{1,0:T(8,128)(2,1)}, f32[8,1536]{1,0:T(8,128)}, f32[8,512]{1,0:T(8,128)}) custom-call(bf16[128,512]{1,0:T(8,128)(2,1)} %bitcast.5, bf16[128,512]{1,0:T(8,128)(2,1)} %bitcast.6, f32[1,512]{1,0:T(1,128)} %bitcast.9, bf16[512,1536]{1,0:T(8,128)(2,1)} %wqkv_hbm.1, bf16[512,512]{1,0:T(8,128)(2,1)} %wout_hbm.1, ...), custom_call_target="tpu_custom_call" | custom-call | flops 1000000000 | bytes 4000000 | tf_op jit(solution)/shard_map/block/pallas_call | solution.py:562
  53.7 1.7 %hand_over.1 = (bf16[128,512]{1,0:T(8,128)(2,1)}, bf16[128,512]{1,0:T(8,128)(2,1)}, f32[8,1536]{1,0:T(8,128)}, f32[8,512]{1,0:T(8,128)}) custom-call(bf16[128,512]{1,0:T(8,128)(2,1)} %get-tuple-element.12.refs_0_, bf16[128,512]{1,0:T(8,128)(2,1)} %get-tuple-element.13.refs_1_, f32[8,1536]{1,0:T(8,128)} %get-tuple-element.14.refs_2_, ...), custom_call_target="tpu_custom_call" | custom-call | tf_op jit(solution)/shard_map/hand_over/pallas_call | solution.py:590

commit v5 on v4

--- a/solution.py
+++ b/solution.py
@@ -87,18 +87,15 @@
         za=v((nz, 4, 16, 128), BF16),
         ryb=v((ny - 1, 8, 16, 128), BF16),
         rzb=v((nz - 1, ny, 16, 128), BF16),
-        syb=v((nz, 16, 128), BF16),
-        szb=v((ny, 16, 128), BF16),
-        r2z=v((nz - 1, 16, 128), BF16),
-        r2y=v((ny - 1, 16, 128), BF16),
-        ub=v((nx, 8, 128), F32),
-        r3x=v((nx - 1, 8, 128), F32),
+        syb=v((2, nz, 8, 128), F32),
+        szb=v((2, ny, 8, 128), F32),
+        mb=v((nx * nz, 8, 128), F32),
         gb=v((nz, 8, 128), F32),
     )
 
 
 def reduce_count(nx, ny, nz):
-    return 2 + 2 * (nx - 1) + 3 * (ny - 1) + 4 * (nz - 1)
+    return 2 + (nx - 1) + 2 * (ny - 1) + 3 * (nz - 1)
 
 
 def core_add(s1, own, got):
@@ -119,7 +116,7 @@
     return xs
 
 
-def reduce_tail(p, links, b, first_b, xs, meanwhile, send_grads, finish, factor, qkv_ref, out_ref):
+def reduce_tail(p, links, b, first_b, xs, owner_sems, meanwhile, send_grads, finish, factor, qkv_ref, out_ref):
     nx, ny, nz = p.nx, p.ny, p.nz
     first_b.wait_recv()
     core_add(b["s1b"], b["own_b"], b["r0b"])
@@ -156,14 +153,39 @@
         total = b["s1b"][p.y, 0, i].astype(F32)
         for k in range(ny - 1):
             total += b["ryb"][k, i].astype(F32)
-        b["syb"][i] = total.astype(BF16)
+        b["syb"][0, i] = total[0:8]
+        b["syb"][1, i] = total[8:16]
         return 0
 
     lax.fori_loop(0, nz, add_y, 0)
-    z3 = []
-    for k in range(1, nz):
-        to, device = p.z_peer(k)
-        z3.append(links.start(b["syb"].at[to], b["r2z"].at[k - 1], device))
+
+    def to_owner(tile, slot, device):
+        return pltpu.make_async_remote_copy(
+            src_ref=tile,
+            dst_ref=b["mb"].at[slot],
+            send_sem=owner_sems.at[0],
+            recv_sem=owner_sems.at[1],
+            device_id=device,
+            device_id_type=pl.DeviceIdType.MESH,
+        )
+
+    def spread(tiles, first, peers, mine):
+        for j in range(2):
+            column = p.gx - p.x + first + j
+            for k in range(peers):
+                if first == 0:
+                    to, device = p.z_peer(k)
+                    device = (p.gy, column, device[2])
+                else:
+                    to, device = p.y_peer(k)
+                    device = (device[0], device[1] - p.x + first + j, p.z)
+                copy = to_owner(tiles.at[j, to], p.x * peers + mine, device)
+                if k > 0:
+                    copy.start()
+                else:
+                    pl.when(p.x != first + j)(copy.start)
+
+    spread(b["syb"], 0, nz, p.z)
 
     for c in zs:
         c.wait_recv()
@@ -172,14 +194,21 @@
         total = b["s1b"][i, 1, p.z].astype(F32)
         for k in range(nz - 1):
             total += b["rzb"][k, i].astype(F32)
-        b["szb"][i] = total.astype(BF16)
+        b["szb"][0, i] = total[0:8]
+        b["szb"][1, i] = total[8:16]
         return 0
 
     lax.fori_loop(0, ny, add_z, 0)
-    y3 = []
-    for k in range(1, ny):
-        to, device = p.y_peer(k)
-        y3.append(links.start(b["szb"].at[to], b["r2y"].at[k - 1], device))
+    spread(b["szb"], 2, ny, p.y)
+
+    @pl.when(p.x < 2)
+    def _():
+        b["mb"][p.x * nz + p.z] = b["syb"][p.x % 2, p.z]
+
+    @pl.when(p.x >= 2)
+    def _():
+        b["mb"][p.x * ny + p.y] = b["szb"][p.x % 2, p.y]
+
     send_grads()
 
     for c in y2:
@@ -193,30 +222,9 @@
         to, device = p.z_peer(k)
         last_a.append(links.start(b["za"].at[p.z], b["za"].at[p.z], device))
 
-    for c in z3:
-        c.wait_recv()
-    low = b["syb"][p.z].astype(F32)
-    for k in range(nz - 1):
-        low += b["r2z"][k].astype(F32)
-    for c in y3:
-        c.wait_recv()
-    high = b["szb"][p.y].astype(F32)
-    for k in range(ny - 1):
-        high += b["r2y"][k].astype(F32)
-    b["ub"][0] = low[0:8]
-    b["ub"][1] = low[8:16]
-    b["ub"][2] = high[0:8]
-    b["ub"][3] = high[8:16]
-    x3 = []
-    for k in range(1, nx):
-        to, device = p.x_peer(k)
-        x3.append(links.start(b["ub"].at[to], b["r3x"].at[k - 1], device))
-
-    for c in x3:
-        c.wait_recv()
-    total = b["ub"][p.x]
-    for k in range(nx - 1):
-        total += b["r3x"][k]
+    others = b["mb"].at[0 : nx * nz - 1]
+    pltpu.make_async_copy(others, others, owner_sems.at[1]).wait()
+    total = jnp.sum(b["mb"][...], axis=0)
     b["gb"][p.z] = total * factor
     last = []
     for k in range(1, nz):
@@ -234,6 +242,7 @@
         out_ref[:, t * 128 : t * 128 + 128] = total[t, 8:16]
     for c in last:
         c.wait_recv()
+    pltpu.make_async_copy(others, others, owner_sems.at[0]).wait()
     for t in range(8):
         qkv_ref[:, 512 + t * 128 : 640 + t * 128] = b["gb"][t]
 
@@ -359,7 +368,7 @@
     def kernel(x_hbm, dy_hbm, gain_ref, wqkv_hbm, wout_hbm, scale_ref, mixed_ref, gin_ref, gqkv_ref, gout_ref, *rest):
         b = dict(zip(names, rest))
         links = Links(*rest[len(names) : len(names) + 2])
-        load_sem = rest[-1]
+        load_sem, owner_sems = rest[len(names) + 2 :]
         x_ref, dy_ref, wqkv_ref, wout_ref = b["x"], b["dy"], b["wqkv"], b["wout"]
         loads = [
             pltpu.make_async_copy(source, target, load_sem.at[i])
@@ -374,7 +383,7 @@
         def neighbour(dy_step, dx_step):
             return ((p.gy + dy_step) % p.ngy, (p.gx + dx_step) % p.ngx, p.z)
 
-        arrive = enter(p.reduce_peers() + [neighbour(*block[3:]) for block in BLOCKS])
+        arrive = enter([neighbour(*block[3:]) for block in BLOCKS] + p.reduce_peers())
 
         def exchange(source, target):
             return [
@@ -555,7 +564,7 @@
             mean = jnp.sum(xf * g, -1, keepdims=True) * (1.0 / 512)
             gin_ref[...] = (dy_ref[...].astype(F32) + inv * g - xf * (inv * inv * inv * mean)).astype(BF16)
 
-        reduce_tail(p, links, b, first_b, xs, meanwhile, send_grads, finish, factor, gqkv_ref, gout_ref)
+        reduce_tail(p, links, b, first_b, xs, owner_sems, meanwhile, send_grads, finish, factor, gqkv_ref, gout_ref)
         links.drain()
 
     vm, anywhere = pl.BlockSpec(memory_space=pltpu.VMEM), pl.BlockSpec(memory_space=pl.ANY)
@@ -570,7 +579,8 @@
         in_specs=[anywhere, anywhere, vm, anywhere, anywhere, pl.BlockSpec(memory_space=pltpu.SMEM)],
         out_specs=(vm, vm, vm, vm),
         scratch_shapes=[scratch[n] for n in names]
-        + [pltpu.SemaphoreType.DMA((count,)), pltpu.SemaphoreType.DMA((count,)), pltpu.SemaphoreType.DMA((4,))],
+        + [pltpu.SemaphoreType.DMA((count,)), pltpu.SemaphoreType.DMA((count,))]
+        + [pltpu.SemaphoreType.DMA((4,)), pltpu.SemaphoreType.DMA((2,))],
         compiler_params=pltpu.CompilerParams(
             collective_id=1, has_side_effects=True, vmem_limit_bytes=56 * 1024 * 1024
         ),

time: 55.9 us -> 54.2 us (0.970)
  Pallas kernels: 54.8 us -> 53.4 us
    pallas_call x1, Pallas kernels: 53.1 us -> 51.7 us  [block_call(): pl.pallas_call(kernel, out_shape=(jax.ShapeDtypeStruct((128, 512), BF16),...]
where the time goes in v5:
time: 54.2 us; the launch traced here: 54 us
  Pallas kernels  53.4 us (99%)
  between operations  0.64 us (1%)
    pallas_call x1, Pallas kernels, block_call(): pl.pallas_call(kernel, out_shape=(jax.ShapeDtypeStruct((128, 512), BF16),...  51.7 us
    pallas_call x1, Pallas kernels, hand_over(): pl.pallas_call(kernel, out_shape=tuple((jax.ShapeDtypeStruct(a.shape, a.d...  1.69 us

profile of v5, /device:TPU:6, one launch (start us, length us, event | category | flops | bytes accessed | tf_op | source)
XLA Modules:
  0.0 54.0 jit_solution(9279929789646284227)
XLA Ops:
  0.6 51.7 %block.1 = (bf16[128,512]{1,0:T(8,128)(2,1)}, bf16[128,512]{1,0:T(8,128)(2,1)}, f32[8,1536]{1,0:T(8,128)}, f32[8,512]{1,0:T(8,128)}) custom-call(bf16[128,512]{1,0:T(8,128)(2,1)} %bitcast.5, bf16[128,512]{1,0:T(8,128)(2,1)} %bitcast.6, f32[1,512]{1,0:T(1,128)} %bitcast.9, bf16[512,1536]{1,0:T(8,128)(2,1)} %wqkv_hbm.1, bf16[512,512]{1,0:T(8,128)(2,1)} %wout_hbm.1, ...), custom_call_target="tpu_custom_call" | custom-call | flops 1000000000 | bytes 4000000 | tf_op jit(solution)/shard_map/block/pallas_call | solution.py:571
  52.3 1.7 %hand_over.1 = (bf16[128,512]{1,0:T(8,128)(2,1)}, bf16[128,512]{1,0:T(8,128)(2,1)}, f32[8,1536]{1,0:T(8,128)}, f32[8,512]{1,0:T(8,128)}) custom-call(bf16[128,512]{1,0:T(8,128)(2,1)} %get-tuple-element.12.refs_0_, bf16[128,512]{1,0:T(8,128)(2,1)} %get-tuple-element.13.refs_1_, f32[8,1536]{1,0:T(8,128)} %get-tuple-element.14.refs_2_, ...), custom_call_target="tpu_custom_call" | custom-call | tf_op jit(solution)/shard_map/hand_over/pallas_call | solution.py:600

commit v6 on v5

--- a/solution.py
+++ b/solution.py
@@ -95,31 +95,37 @@
 
 
 def reduce_count(nx, ny, nz):
-    return 2 + (nx - 1) + 2 * (ny - 1) + 3 * (nz - 1)
-
-
-def core_add(s1, own, got):
+    return 3 + 2 * (nx - 1) + 3 * (ny - 1) + 4 * (nz - 1)
+
+
+def core_add(s1, own, got, tiles):
     def add(i, _):
-        s1[i] = (own[i].astype(F32) + got[i].astype(F32)).astype(BF16)
+        s1[i, :, tiles] = (own[i, :, tiles].astype(F32) + got[i, :, tiles].astype(F32)).astype(BF16)
         return 0
 
     lax.fori_loop(0, s1.shape[0], add, 0)
 
 
-def start_a(p, links, b, first_a):
-    first_a.wait_recv()
-    core_add(b["s1a"], b["own_a"], b["r0a"])
+CHUNKS = (slice(0, 2), slice(2, 4))
+
+
+def start_a(p, links, b, firsts):
     xs = []
-    for k in range(1, p.nx):
-        to, device = p.x_peer(k)
-        xs.append(links.start(b["s1a"].at[:, to], b["rxa"].at[k - 1], device))
+    for first, tiles in zip(firsts, CHUNKS):
+        first.wait_recv()
+        core_add(b["s1a"], b["own_a"], b["r0a"], tiles)
+        sent = []
+        for k in range(1, p.nx):
+            to, device = p.x_peer(k)
+            sent.append(links.start(b["s1a"].at[:, to, tiles], b["rxa"].at[k - 1, :, tiles], device))
+        xs.append(sent)
     return xs
 
 
-def reduce_tail(p, links, b, first_b, xs, owner_sems, meanwhile, send_grads, finish, factor, qkv_ref, out_ref):
+def reduce_tail(p, links, b, first_b, first_a, owner_sems, meanwhile, send_grads, finish, factor, qkv_ref, out_ref):
     nx, ny, nz = p.nx, p.ny, p.nz
     first_b.wait_recv()
-    core_add(b["s1b"], b["own_b"], b["r0b"])
+    core_add(b["s1b"], b["own_b"], b["r0b"], slice(0, 8))
     ys, zs = [], []
     for k in range(1, max(ny, nz)):
         if k < ny:
@@ -128,23 +134,27 @@
         if k < nz:
             to, device = p.z_peer(k)
             zs.append(links.start(b["s1b"].at[:, 1, to], b["rzb"].at[k - 1], device))
+    xs = start_a(p, links, b, first_a)
     meanwhile()
 
-    for c in xs:
-        c.wait_recv()
-
-    def add_x(i, _):
-        total = b["s1a"][i, p.x].astype(F32)
-        for k in range(nx - 1):
-            total += b["rxa"][k, i].astype(F32)
-        b["s2a"][i] = total.astype(BF16)
-        return 0
-
-    lax.fori_loop(0, ny, add_x, 0)
     y2 = []
-    for k in range(1, ny):
-        to, device = p.y_peer(k)
-        y2.append(links.start(b["s2a"].at[to], b["rya"].at[k - 1], device))
+    for arriving, tiles in zip(xs, CHUNKS):
+        for c in arriving:
+            c.wait_recv()
+
+        def add_x(i, _):
+            total = b["s1a"][i, p.x, tiles].astype(F32)
+            for k in range(nx - 1):
+                total += b["rxa"][k, i, tiles].astype(F32)
+            b["s2a"][i, tiles] = total.astype(BF16)
+            return 0
+
+        lax.fori_loop(0, ny, add_x, 0)
+        sent = []
+        for k in range(1, ny):
+            to, device = p.y_peer(k)
+            sent.append(links.start(b["s2a"].at[to, tiles], b["rya"].at[k - 1, tiles], device))
+        y2.append(sent)
 
     for c in ys:
         c.wait_recv()
@@ -211,16 +221,17 @@
 
     send_grads()
 
-    for c in y2:
-        c.wait_recv()
-    total = b["s2a"][p.y].astype(F32)
-    for k in range(ny - 1):
-        total += b["rya"][k].astype(F32)
-    b["za"][p.z] = total.astype(BF16)
     last_a = []
-    for k in range(1, nz):
-        to, device = p.z_peer(k)
-        last_a.append(links.start(b["za"].at[p.z], b["za"].at[p.z], device))
+    for arriving, tiles in zip(y2, CHUNKS):
+        for c in arriving:
+            c.wait_recv()
+        total = b["s2a"][p.y, tiles].astype(F32)
+        for k in range(ny - 1):
+            total += b["rya"][k, tiles].astype(F32)
+        b["za"][p.z, tiles] = total.astype(BF16)
+        for k in range(1, nz):
+            to, device = p.z_peer(k)
+            last_a.append(links.start(b["za"].at[p.z, tiles], b["za"].at[p.z, tiles], device))
 
     others = b["mb"].at[0 : nx * nz - 1]
     pltpu.make_async_copy(others, others, owner_sems.at[1]).wait()
@@ -491,31 +502,8 @@
             b["ds_h"][i] = ds_h
             b["p_l"][i] = probs
             b["ds_l"][i] = ds
-            att_t = pick(dot(b["kv"][:, more], probs, FIRST) + dot(b["halo"][:, more], probs_h, FIRST))
-            gqs_t = pick(dot(b["kv"][:, lanes], ds, FIRST) + dot(b["halo"][:, lanes], ds_h, FIRST))
-            b["att_t"][i] = att_t.astype(BF16).reshape(2, 64, 128)
-            b["att"][:, lanes] = att_t.T.astype(BF16)
-            gqs = gqs_t.T
-            uq = b["uq"][:, lanes]
-            b["act"][:, lanes] = (b["nq"][:, lanes] * (gqs - uq * head_sum(uq * gqs, ones))).astype(BF16)
 
         rows = 32 * ny
-
-        def part_a(core):
-            q_part = dot(b["normed_t"][:, core].reshape(rows, 128), b["act"][:, 0:512])
-            out_part = dot(b["att_t"][:, core].reshape(rows, 128), dy_ref[...])
-            return [
-                jnp.concatenate(
-                    [a[:, t * 128 : t * 128 + 128].reshape(ny, nx, 8, 128) for a in (q_part, out_part)], axis=2
-                )
-                for t in range(4)
-            ]
-
-        for t, tile in enumerate(part_a(1 - p.core)):
-            b["s0a"][:, :, t] = tile.astype(BF16)
-        first_a = links.start(b["s0a"], b["r0a"], p.other_core())
-        for t, tile in enumerate(part_a(p.core)):
-            b["own_a"][:, :, t] = tile
 
         for i in range(4):
             lanes, more = slice(i * 128, i * 128 + 128), slice(512 + i * 128, 640 + i * 128)
@@ -529,12 +517,42 @@
             a += dot(b["normed_th"][:, core].reshape(rows, 224), b["act_h"][...])
             return [a[:, t * 128 : t * 128 + 128].reshape(ny, 2, 16, 128) for t in range(8)]
 
-        xs = start_a(p, links, b, first_a)
         for t, tile in enumerate(part_b(1 - p.core)):
             b["s0b"][:, :, t] = tile.astype(BF16)
         first_b = links.start(b["s0b"], b["r0b"], p.other_core())
         for t, tile in enumerate(part_b(p.core)):
             b["own_b"][:, :, t] = tile
+
+        for i in range(4):
+            lanes, more = slice(i * 128, i * 128 + 128), slice(512 + i * 128, 640 + i * 128)
+            att_t = pick(dot(b["kv"][:, more], b["p_l"][i], FIRST) + dot(b["halo"][:, more], b["p_h"][i], FIRST))
+            gqs_t = pick(dot(b["kv"][:, lanes], b["ds_l"][i], FIRST) + dot(b["halo"][:, lanes], b["ds_h"][i], FIRST))
+            b["att_t"][i] = att_t.astype(BF16).reshape(2, 64, 128)
+            b["att"][:, lanes] = att_t.T.astype(BF16)
+            gqs = gqs_t.T
+            uq = b["uq"][:, lanes]
+            b["act"][:, lanes] = (b["nq"][:, lanes] * (gqs - uq * head_sum(uq * gqs, ones))).astype(BF16)
+
+        def part_a(core, tiles):
+            lanes = slice(tiles.start * 128, tiles.stop * 128)
+            q_part = dot(b["normed_t"][:, core].reshape(rows, 128), b["act"][:, lanes])
+            out_part = dot(b["att_t"][:, core].reshape(rows, 128), dy_ref[:, lanes])
+            return [
+                jnp.concatenate(
+                    [a[:, t * 128 : t * 128 + 128].reshape(ny, nx, 8, 128) for a in (q_part, out_part)], axis=2
+                )
+                for t in range(tiles.stop - tiles.start)
+            ]
+
+        first_a = []
+        for tiles in CHUNKS:
+            for t, tile in enumerate(part_a(1 - p.core, tiles)):
+                b["s0a"][:, :, tiles.start + t] = tile.astype(BF16)
+            first_a.append(links.start(b["s0a"].at[:, :, tiles], b["r0a"].at[:, :, tiles], p.other_core()))
+        for tiles in CHUNKS:
+            for t, tile in enumerate(part_a(p.core, tiles)):
+                b["own_a"][:, :, tiles.start + t] = tile
+
         grads = []
 
         def send_grads():
@@ -564,7 +582,7 @@
             mean = jnp.sum(xf * g, -1, keepdims=True) * (1.0 / 512)
             gin_ref[...] = (dy_ref[...].astype(F32) + inv * g - xf * (inv * inv * inv * mean)).astype(BF16)
 
-        reduce_tail(p, links, b, first_b, xs, owner_sems, meanwhile, send_grads, finish, factor, gqkv_ref, gout_ref)
+        reduce_tail(p, links, b, first_b, first_a, owner_sems, meanwhile, send_grads, finish, factor, gqkv_ref, gout_ref)
         links.drain()
 
     vm, anywhere = pl.BlockSpec(memory_space=pltpu.VMEM), pl.BlockSpec(memory_space=pl.ANY)

time: 54.2 us -> 52.3 us (0.965)
  Pallas kernels: 53.4 us -> 51.5 us
    pallas_call x1, Pallas kernels: 51.7 us -> 49.8 us  [block_call(): pl.pallas_call(kernel, out_shape=(jax.ShapeDtypeStruct((128, 512), BF16),...]
where the time goes in v6:
time: 52.3 us; the launch traced here: 52.2 us
  Pallas kernels  51.5 us (98%)
  between operations  0.64 us (1%)
    pallas_call x1, Pallas kernels, block_call(): pl.pallas_call(kernel, out_shape=(jax.ShapeDtypeStruct((128, 512), BF16),...  49.8 us
    pallas_call x1, Pallas kernels, hand_over(): pl.pallas_call(kernel, out_shape=tuple((jax.ShapeDtypeStruct(a.shape, a.d...  1.69 us

profile of v6, /device:TPU:6, one launch (start us, length us, event | category | flops | bytes accessed | tf_op | source)
XLA Modules:
  0.0 52.2 jit_solution(18387312436396189646)
XLA Ops:
  0.6 49.8 %block.1 = (bf16[128,512]{1,0:T(8,128)(2,1)}, bf16[128,512]{1,0:T(8,128)(2,1)}, f32[8,1536]{1,0:T(8,128)}, f32[8,512]{1,0:T(8,128)}) custom-call(bf16[128,512]{1,0:T(8,128)(2,1)} %bitcast.5, bf16[128,512]{1,0:T(8,128)(2,1)} %bitcast.6, f32[1,512]{1,0:T(1,128)} %bitcast.9, bf16[512,1536]{1,0:T(8,128)(2,1)} %wqkv_hbm.1, bf16[512,512]{1,0:T(8,128)(2,1)} %wout_hbm.1, ...), custom_call_target="tpu_custom_call" | custom-call | flops 1000000000 | bytes 4000000 | tf_op jit(solution)/shard_map/block/pallas_call | solution.py:589
  50.5 1.7 %hand_over.1 = (bf16[128,512]{1,0:T(8,128)(2,1)}, bf16[128,512]{1,0:T(8,128)(2,1)}, f32[8,1536]{1,0:T(8,128)}, f32[8,512]{1,0:T(8,128)}) custom-call(bf16[128,512]{1,0:T(8,128)(2,1)} %get-tuple-element.12.refs_0_, bf16[128,512]{1,0:T(8,128)(2,1)} %get-tuple-element.13.refs_1_, f32[8,1536]{1,0:T(8,128)} %get-tuple-element.14.refs_2_, ...), custom_call_target="tpu_custom_call" | custom-call | tf_op jit(solution)/shard_map/hand_over/pallas_call | solution.py:618

commit v7 on v6

--- a/solution.py
+++ b/solution.py
@@ -95,7 +95,7 @@
 
 
 def reduce_count(nx, ny, nz):
-    return 3 + 2 * (nx - 1) + 3 * (ny - 1) + 4 * (nz - 1)
+    return 4 + 2 * (nx - 1) + 3 * (ny - 1) + 4 * (nz - 1)
 
 
 def core_add(s1, own, got, tiles):
@@ -107,6 +107,7 @@
 
 
 CHUNKS = (slice(0, 2), slice(2, 4))
+HALVES = (slice(4, 8), slice(0, 4))
 
 
 def start_a(p, links, b, firsts):
@@ -115,25 +116,32 @@
         first.wait_recv()
         core_add(b["s1a"], b["own_a"], b["r0a"], tiles)
         sent = []
-        for k in range(1, p.nx):
+        for k in far_first(p.nx):
             to, device = p.x_peer(k)
             sent.append(links.start(b["s1a"].at[:, to, tiles], b["rxa"].at[k - 1, :, tiles], device))
         xs.append(sent)
     return xs
 
 
-def reduce_tail(p, links, b, first_b, first_a, owner_sems, meanwhile, send_grads, finish, factor, qkv_ref, out_ref):
+def far_first(n):
+    return sorted(range(1, n), key=lambda k: -min(k, n - k))
+
+
+def start_b(p, links, b, firsts):
+    for first, tiles in zip(firsts, HALVES):
+        first.wait_recv()
+        core_add(b["s1b"], b["own_b"], b["r0b"], tiles)
+    ys, zs = [], []
+    for k in far_first(p.ny):
+        to, device = p.y_peer(k)
+        ys.append(links.start(b["s1b"].at[to, 0], b["ryb"].at[k - 1], device))
+        to, device = p.z_peer(k)
+        zs.append(links.start(b["s1b"].at[:, 1, to], b["rzb"].at[k - 1], device))
+    return ys, zs
+
+
+def reduce_tail(p, links, b, ys, zs, first_a, owner_sems, meanwhile, send_grads, finish, factor, qkv_ref, out_ref):
     nx, ny, nz = p.nx, p.ny, p.nz
-    first_b.wait_recv()
-    core_add(b["s1b"], b["own_b"], b["r0b"], slice(0, 8))
-    ys, zs = [], []
-    for k in range(1, max(ny, nz)):
-        if k < ny:
-            to, device = p.y_peer(k)
-            ys.append(links.start(b["s1b"].at[to, 0], b["ryb"].at[k - 1], device))
-        if k < nz:
-            to, device = p.z_peer(k)
-            zs.append(links.start(b["s1b"].at[:, 1, to], b["rzb"].at[k - 1], device))
     xs = start_a(p, links, b, first_a)
     meanwhile()
 
@@ -151,7 +159,7 @@
 
         lax.fori_loop(0, ny, add_x, 0)
         sent = []
-        for k in range(1, ny):
+        for k in far_first(ny):
             to, device = p.y_peer(k)
             sent.append(links.start(b["s2a"].at[to, tiles], b["rya"].at[k - 1, tiles], device))
         y2.append(sent)
@@ -182,7 +190,7 @@
     def spread(tiles, first, peers, mine):
         for j in range(2):
             column = p.gx - p.x + first + j
-            for k in range(peers):
+            for k in far_first(peers) + [0]:
                 if first == 0:
                     to, device = p.z_peer(k)
                     device = (p.gy, column, device[2])
@@ -229,7 +237,7 @@
         for k in range(ny - 1):
             total += b["rya"][k, tiles].astype(F32)
         b["za"][p.z, tiles] = total.astype(BF16)
-        for k in range(1, nz):
+        for k in far_first(nz):
             to, device = p.z_peer(k)
             last_a.append(links.start(b["za"].at[p.z, tiles], b["za"].at[p.z, tiles], device))
 
@@ -238,7 +246,7 @@
     total = jnp.sum(b["mb"][...], axis=0)
     b["gb"][p.z] = total * factor
     last = []
-    for k in range(1, nz):
+    for k in far_first(nz):
         to, device = p.z_peer(k)
         last.append(links.start(b["gb"].at[p.z], b["gb"].at[p.z], device))
     finish()
@@ -505,23 +513,30 @@
 
         rows = 32 * ny
 
+        def part_b(core, tiles):
+            lanes = slice(tiles.start * 128, tiles.stop * 128)
+            a = dot(b["normed_t"][:, core].reshape(rows, 128), b["act"][:, 512 + lanes.start : 512 + lanes.stop])
+            a += dot(b["normed_th"][:, core].reshape(rows, 224), b["act_h"][:, lanes])
+            return [(tiles.start + t, a[:, t * 128 : t * 128 + 128].reshape(ny, 2, 16, 128)) for t in range(4)]
+
+        def send_b(tiles):
+            for t, tile in part_b(1 - p.core, tiles):
+                b["s0b"][:, :, t] = tile.astype(BF16)
+            return links.start(b["s0b"].at[:, :, tiles], b["r0b"].at[:, :, tiles], p.other_core())
+
+        for i in range(4):
+            more = slice(512 + i * 128, 640 + i * 128)
+            b["act_h"][:, more] = dot(b["p_h"][i], b["gm"][i]).astype(BF16)
+            b["act"][:, 1024 + i * 128 : 1152 + i * 128] = dot(b["p_l"][i], b["gm"][i]).astype(BF16)
+        first_b = [send_b(HALVES[0])]
         for i in range(4):
             lanes, more = slice(i * 128, i * 128 + 128), slice(512 + i * 128, 640 + i * 128)
             b["act_h"][:, lanes] = key_gradient(b["uk_h"][:, lanes], b["nk_h"][:, lanes], dot(b["ds_h"][i], b["qm"][i]))
-            b["act_h"][:, more] = dot(b["p_h"][i], b["gm"][i]).astype(BF16)
             b["act"][:, more] = key_gradient(b["uk"][:, lanes], b["nk"][:, lanes], dot(b["ds_l"][i], b["qm"][i]))
-            b["act"][:, 1024 + i * 128 : 1152 + i * 128] = dot(b["p_l"][i], b["gm"][i]).astype(BF16)
-
-        def part_b(core):
-            a = dot(b["normed_t"][:, core].reshape(rows, 128), b["act"][:, 512:1536])
-            a += dot(b["normed_th"][:, core].reshape(rows, 224), b["act_h"][...])
-            return [a[:, t * 128 : t * 128 + 128].reshape(ny, 2, 16, 128) for t in range(8)]
-
-        for t, tile in enumerate(part_b(1 - p.core)):
-            b["s0b"][:, :, t] = tile.astype(BF16)
-        first_b = links.start(b["s0b"], b["r0b"], p.other_core())
-        for t, tile in enumerate(part_b(p.core)):
-            b["own_b"][:, :, t] = tile
+        first_b.append(send_b(HALVES[1]))
+        for tiles in HALVES:
+            for t, tile in part_b(p.core, tiles):
+                b["own_b"][:, :, t] = tile
 
         for i in range(4):
             lanes, more = slice(i * 128, i * 128 + 128), slice(512 + i * 128, 640 + i * 128)
@@ -549,6 +564,7 @@
             for t, tile in enumerate(part_a(1 - p.core, tiles)):
                 b["s0a"][:, :, tiles.start + t] = tile.astype(BF16)
             first_a.append(links.start(b["s0a"].at[:, :, tiles], b["r0a"].at[:, :, tiles], p.other_core()))
+        ys, zs = start_b(p, links, b, first_b)
         for tiles in CHUNKS:
             for t, tile in enumerate(part_a(p.core, tiles)):
                 b["own_a"][:, :, tiles.start + t] = tile
@@ -582,7 +598,7 @@
             mean = jnp.sum(xf * g, -1, keepdims=True) * (1.0 / 512)
             gin_ref[...] = (dy_ref[...].astype(F32) + inv * g - xf * (inv * inv * inv * mean)).astype(BF16)
 
-        reduce_tail(p, links, b, first_b, first_a, owner_sems, meanwhile, send_grads, finish, factor, gqkv_ref, gout_ref)
+        reduce_tail(p, links, b, ys, zs, first_a, owner_sems, meanwhile, send_grads, finish, factor, gqkv_ref, gout_ref)
         links.drain()
 
     vm, anywhere = pl.BlockSpec(memory_space=pltpu.VMEM), pl.BlockSpec(memory_space=pl.ANY)

time: 52.3 us -> 51.2 us (0.979)
  Pallas kernels: 51.5 us -> 50.4 us
    pallas_call x1, Pallas kernels: 49.8 us -> 48.7 us  [block_call(): pl.pallas_call(kernel, out_shape=(jax.ShapeDtypeStruct((128, 512), BF16),...]
where the time goes in v7:
time: 51.2 us; the launch traced here: 51.1 us
  Pallas kernels  50.4 us (98%)
  between operations  0.64 us (1%)
    pallas_call x1, Pallas kernels, block_call(): pl.pallas_call(kernel, out_shape=(jax.ShapeDtypeStruct((128, 512), BF16),...  48.7 us
    pallas_call x1, Pallas kernels, hand_over(): pl.pallas_call(kernel, out_shape=tuple((jax.ShapeDtypeStruct(a.shape, a.d...  1.69 us

profile of v7, /device:TPU:6, one launch (start us, length us, event | category | flops | bytes accessed | tf_op | source)
XLA Modules:
  0.0 51.1 jit_solution(16467385931393858586)
XLA Ops:
  0.6 48.7 %block.1 = (bf16[128,512]{1,0:T(8,128)(2,1)}, bf16[128,512]{1,0:T(8,128)(2,1)}, f32[8,1536]{1,0:T(8,128)}, f32[8,512]{1,0:T(8,128)}) custom-call(bf16[128,512]{1,0:T(8,128)(2,1)} %bitcast.5, bf16[128,512]{1,0:T(8,128)(2,1)} %bitcast.6, f32[1,512]{1,0:T(1,128)} %bitcast.9, bf16[512,1536]{1,0:T(8,128)(2,1)} %wqkv_hbm.1, bf16[512,512]{1,0:T(8,128)(2,1)} %wout_hbm.1, ...), custom_call_target="tpu_custom_call" | custom-call | flops 1000000000 | bytes 4000000 | tf_op jit(solution)/shard_map/block/pallas_call | solution.py:605
  49.4 1.7 %hand_over.1 = (bf16[128,512]{1,0:T(8,128)(2,1)}, bf16[128,512]{1,0:T(8,128)(2,1)}, f32[8,1536]{1,0:T(8,128)}, f32[8,512]{1,0:T(8,128)}) custom-call(bf16[128,512]{1,0:T(8,128)(2,1)} %get-tuple-element.12.refs_0_, bf16[128,512]{1,0:T(8,128)(2,1)} %get-tuple-element.13.refs_1_, f32[8,1536]{1,0:T(8,128)} %get-tuple-element.14.refs_2_, ...), custom_call_target="tpu_custom_call" | custom-call | tf_op jit(solution)/shard_map/hand_over/pallas_call | solution.py:634

commit v8 on v7

--- a/solution.py
+++ b/solution.py
@@ -324,14 +324,14 @@
 
 
 BLOCKS = (
-    (0, 48, 48, -1, 0),
-    (48, 48, 0, 1, 0),
-    (96, 32, 128, 0, -1),
-    (128, 32, 96, 0, 1),
     (160, 16, 208, -1, -1),
     (176, 16, 192, -1, 1),
     (192, 16, 176, 1, -1),
     (208, 16, 160, 1, 1),
+    (96, 32, 128, 0, -1),
+    (128, 32, 96, 0, 1),
+    (0, 48, 48, -1, 0),
+    (48, 48, 0, 1, 0),
 )
 
 

time: 51.2 us -> 50.5 us (0.986)
  Pallas kernels: 50.4 us -> 49.7 us
    pallas_call x1, Pallas kernels: 48.7 us -> 48 us  [block_call(): pl.pallas_call(kernel, out_shape=(jax.ShapeDtypeStruct((128, 512), BF16),...]
where the time goes in v8:
time: 50.5 us; the launch traced here: 50.3 us
  Pallas kernels  49.7 us (98%)
  between operations  0.64 us (1%)
    pallas_call x1, Pallas kernels, block_call(): pl.pallas_call(kernel, out_shape=(jax.ShapeDtypeStruct((128, 512), BF16),...  48 us
    pallas_call x1, Pallas kernels, hand_over(): pl.pallas_call(kernel, out_shape=tuple((jax.ShapeDtypeStruct(a.shape, a.d...  1.69 us

profile of v8, /device:TPU:6, one launch (start us, length us, event | category | flops | bytes accessed | tf_op | source)
XLA Modules:
  0.0 50.3 jit_solution(15392523644438162871)
XLA Ops:
  0.6 48.0 %block.1 = (bf16[128,512]{1,0:T(8,128)(2,1)}, bf16[128,512]{1,0:T(8,128)(2,1)}, f32[8,1536]{1,0:T(8,128)}, f32[8,512]{1,0:T(8,128)}) custom-call(bf16[128,512]{1,0:T(8,128)(2,1)} %bitcast.5, bf16[128,512]{1,0:T(8,128)(2,1)} %bitcast.6, f32[1,512]{1,0:T(1,128)} %bitcast.9, bf16[512,1536]{1,0:T(8,128)(2,1)} %wqkv_hbm.1, bf16[512,512]{1,0:T(8,128)(2,1)} %wout_hbm.1, ...), custom_call_target="tpu_custom_call" | custom-call | flops 1000000000 | bytes 4000000 | tf_op jit(solution)/shard_map/block/pallas_call | solution.py:605
  48.6 1.7 %hand_over.1 = (bf16[128,512]{1,0:T(8,128)(2,1)}, bf16[128,512]{1,0:T(8,128)(2,1)}, f32[8,1536]{1,0:T(8,128)}, f32[8,512]{1,0:T(8,128)}) custom-call(bf16[128,512]{1,0:T(8,128)(2,1)} %get-tuple-element.12.refs_0_, bf16[128,512]{1,0:T(8,128)(2,1)} %get-tuple-element.13.refs_1_, f32[8,1536]{1,0:T(8,128)} %get-tuple-element.14.refs_2_, ...), custom_call_target="tpu_custom_call" | custom-call | tf_op jit(solution)/shard_map/hand_over/pallas_call | solution.py:634
